TPU v7x, 128 devices: a whole 4x4x4 slice. The times are simulated.
128 devices in a mesh: grp: 4 (over x), tile: 32 (over y, z, core).
Axes of the slice: x: 4, y: 4, z: 4, core: 2. Of those that a mesh axis runs over, the one named last changes fastest.
Arguments:
- state: float32 [64, 1024, 512], P(None, ('grp', 'tile')), may hold values from -6 to 6
- vert_coef: float32 [63, 1024, 512], P(None, ('grp', 'tile')), may hold values from 0.0004 to 1200
- horiz_coef: float32 [1024, 512], P(('grp', 'tile')), may hold values from 0.02 to 0.24
- wet_mask: int32 [256, 512], P('tile'), may hold values 0 or 1
- coupling: float32 [4, 1024, 512], P(None, ('grp', 'tile')), may hold values from 0.1 to 1
- surface_in: float32 [4, 1024, 512], P(None, ('grp', 'tile')), may hold values from -6 to 6
- remap_w: bfloat16 [4096, 4, 128, 128], P(('grp', 'tile')), may hold values from -0.25 to 0.25
- dest_tile: int32 [4096, 4], P(('grp', 'tile')), may hold values from 0 to 31, all different within a row; in each aligned block of 32 rows (0 to 31, 32 to 63, ...) at most 8 rows name the same one
- dest_block: int32 [4096, 4], P(('grp', 'tile')), may hold values from 0 to 31
- dest_group: int32 [4096, 4], P(('grp', 'tile')), may hold values from 0 to 2
Outputs:
- state_out: float32 [64, 1024, 512], P(None, ('grp', 'tile'))
- received: float32 [4, 1024, 512], P(None, ('grp', 'tile'))
Inputs may be any that keep to these rules, and one draw needn't show every extreme that they name: `dest_tile`: A row's 4 strip indices differ; within the 32 rows of one device no strip index appears more than 8 times, and some device reaches 8.
All inputs are finite; a program needn't handle non-finite values. No bound on the sum of `wet_mask` on one device may be relied on, other than what follows from the above.
Results may differ from a plain program's by a relative error of at most 0.0029.
Values sent between devices are 32-bit elements; how exact they have to be, the bound alone decides.
A program may use at most 64 MiB of HBM per device.

v0:
```python
import jax
import jax.numpy as jnp
from jax import lax
from jax.sharding import PartitionSpec as P

F = 4
K = 4
STEPS = 2


FORCING_GAIN = 0.25


def padded_2(block, sides, width):
    for axis, dim in sides:
        count = lax.axis_size(axis)
        forward = [(i, i + 1) for i in range(count - 1)]
        backward = [(target, source) for source, target in forward]
        low = lax.ppermute(
            lax.slice_in_dim(block, block.shape[dim] - width, None, axis=dim), axis, forward
        )
        high = lax.ppermute(lax.slice_in_dim(block, 0, width, axis=dim), axis, backward)
        block = jnp.concatenate([low, block, high], axis=dim)
    return block


def vertical_solve(column_rhs, lower, upper):

    def forward(carry, items):
        c_prev, r_prev = carry
        low, upp, rhs = items
        denom = 1.0 + low + upp + low * c_prev
        c_now = -upp / denom
        r_now = (rhs + low * r_prev) / denom
        return ((c_now, r_now), (c_now, r_now))

    zero = jnp.zeros(column_rhs.shape[1:], jnp.float32)
    _, (c_all, r_all) = lax.scan(forward, (zero, zero), (lower, upper, column_rhs), unroll=True)

    def backward(x_next, items):
        c_now, r_now = items
        x_now = r_now - c_now * x_next
        return (x_now, x_now)

    _, solved = lax.scan(backward, zero, (c_all, r_all), reverse=True, unroll=True)
    return solved


def horizontal(field, nu, wet, above, below, wet_above, wet_underneath, keep_above, keep_below):
    left = jnp.pad(field[:, :, :-1], ((0, 0), (0, 0), (1, 0)))
    right = jnp.pad(field[:, :, 1:], ((0, 0), (0, 0), (0, 1)))
    wet_left = jnp.pad(wet[:, :-1], ((0, 0), (1, 0)))
    wet_right = jnp.pad(wet[:, 1:], ((0, 0), (0, 1)))
    total = wet_left * (left - field) + wet_right * (right - field)
    total = (
        total
        + keep_above * wet_above * (above - field)
        + keep_below * wet_underneath * (below - field)
    )
    return field + nu * wet * total


def place_terms(terms, bucket, label, bucket_slots, slots):
    hits = (bucket[:, None] == jnp.arange(bucket_slots, dtype=jnp.int32)[None, :]).astype(jnp.int32)
    before = jnp.cumsum(hits, 0) - hits
    position = jnp.sum(before * hits, 1)
    slot_id = bucket * slots + position
    chooser = (
        slot_id[None, :] == jnp.arange(bucket_slots * slots, dtype=jnp.int32)[:, None]
    ).astype(jnp.float32)
    packed = jnp.dot(chooser, terms, precision=lax.Precision.HIGHEST)
    tags = jnp.dot(chooser, (label + 1).astype(jnp.float32), precision=lax.Precision.HIGHEST) - 1.0
    return (packed, tags)


def local(
    state,
    vert_coef,
    horiz_coef,
    wet_mask,
    coupling,
    surface_in,
    remap_w,
    dest_tile,
    dest_block,
    dest_group,
):
    levels, height, width = state.shape
    groups = lax.axis_size("grp")
    tiles = lax.axis_size("tile")
    group_id = lax.axis_index("grp")
    device_id = group_id * tiles + lax.axis_index("tile")
    ocean = group_id == 3
    ocean_start = 3 * tiles * height
    total_rows = groups * tiles * height
    wet = jnp.where(ocean, wet_mask.astype(jnp.float32), jnp.ones((height, width), jnp.float32))
    blocks = height * width // 128
    slots = max(2, 2 * blocks * K // tiles)
    send = (coupling * (state[0][None] - surface_in) * wet[None]).astype(jnp.bfloat16)
    send = send.reshape(F, blocks, 128).transpose(1, 0, 2)
    terms = jnp.einsum("bfi,bkij->bkfj", send, remap_w, preferred_element_type=jnp.float32)
    terms = terms.reshape(blocks * K, F * 128)
    tile_flat = dest_tile.reshape(-1)
    block_flat = dest_block.reshape(-1)
    group_flat = jnp.where(ocean, dest_group, 3).reshape(-1)
    packed, tags = place_terms(
        terms, group_flat * tiles + tile_flat, block_flat, groups * tiles, slots
    )
    got, got_tags = (
        lax.all_to_all(
            packed.reshape(groups * tiles, slots, F * 128),
            ("grp", "tile"),
            split_axis=0,
            concat_axis=0,
            tiled=True,
        ),
        lax.all_to_all(
            tags.reshape(groups * tiles, slots),
            ("grp", "tile"),
            split_axis=0,
            concat_axis=0,
            tiled=True,
        ),
    )
    requested_items = jnp.arange(blocks, dtype=jnp.int32).astype(jnp.float32)
    chooser = (got_tags.reshape(-1)[None, :] == requested_items[:, None]).astype(jnp.float32)
    gathered = jnp.dot(chooser, got.reshape(-1, F * 128), precision=lax.Precision.HIGHEST)
    received = gathered.reshape(blocks, F, 128).transpose(1, 0, 2).reshape(F, height, width)
    row_ids = device_id * height + jnp.arange(height, dtype=jnp.int32)
    keep_above = ((row_ids > 0) & (row_ids != ocean_start)).astype(jnp.float32)[:, None]
    keep_below = ((row_ids < total_rows - 1) & (row_ids + 1 != ocean_start)).astype(jnp.float32)[
        :, None
    ]
    forcing = FORCING_GAIN * wet * jnp.sum(received, 0)
    scaled = vert_coef * wet[None]
    edge = jnp.zeros((1, height, width), jnp.float32)
    lower = jnp.concatenate([edge, scaled], 0)
    upper = jnp.concatenate([scaled, edge], 0)
    field = state
    for step in range(STEPS):
        stacked = jnp.concatenate([field, wet[None]], 0)
        padded = padded_2(stacked, ((("grp", "tile"), 1),), 1)
        above = padded[:levels, :-2]
        below = padded[:levels, 2:]
        wet_above = padded[levels, :-2]
        wet_underneath = padded[levels, 2:]
        field = horizontal(
            field, horiz_coef, wet, above, below, wet_above, wet_underneath, keep_above, keep_below
        )
        field = field.at[0].add(forcing)
        field = vertical_solve(field, lower, upper)
    return (field, received)


def solution(mesh):
    in_specs = (
        P(None, ("grp", "tile"), None),
        P(None, ("grp", "tile"), None),
        P(("grp", "tile"), None),
        P("tile", None),
        P(None, ("grp", "tile"), None),
        P(None, ("grp", "tile"), None),
        P(("grp", "tile"), None, None, None),
        P(("grp", "tile"), None),
        P(("grp", "tile"), None),
        P(("grp", "tile"), None),
    )
    out_specs = (P(None, ("grp", "tile"), None), P(None, ("grp", "tile"), None))
    return jax.shard_map(local, mesh=mesh, in_specs=in_specs, out_specs=out_specs, check_vma=False)
```

profile of v0, /device:TPU:6, one launch (start us, length us, event | category | flops | bytes accessed | tf_op | source)
XLA Modules:
  0.0 110.0 jit_solution(11108270745552220269)
XLA Ops:
  0.7 1.3 %fusion.440 = (f32[8,512]{1,0:T(8,128)}, f32[8,512]{1,0:T(8,128)S(1)}) fusion(f32[8,512]{1,0:T(8,128)} %param.16, s32[8,512]{1,0:T(8,128)} %param.17, pred[]{:T(512)S(6)} %eq.61), kind=kLoop, calls=%fused_computation.1353 | loop fusion | flops 12288 | bytes 65537 | tf_op jit(solution)/shard_map/mul | solution.py:60
  2.0 1.9 %pad_maximum_fusion.7 = (f32[65,1,512]{2,1,0:T(1,128)S(1)}, f32[65,1,512]{2,1,0:T(1,128)S(1)}) fusion(f32[1,8,512]{2,1,0:T(8,128)S(1)} %bitcast.3015, f32[64,8,512]{2,1,0:T(8,128)} %param.14), kind=kLoop, calls=%fused_computation.225 | loop fusion | flops 66560 | bytes 1331200 | tf_op jit(solution)/shard_map/slice | solution.py:20
  3.9 1.9 %collective-permute-start = (f32[65,1,512]{2,1,0:T(1,128)S(1)}, f32[65,1,512]{2,1,0:T(1,128)S(1)}, u32[]{:S(2)}, u32[]{:S(2)}) collective-permute-start(f32[65,1,512]{2,1,0:T(1,128)S(1)} %get-tuple-element.431), channel_id=1, source_target_pairs={{0,1},{1,2},{2,3},{3,4},{4,5},{5,6},{6,7},{7,8},{8,9},{9,10},{10,1... | collective-permute-start | bytes 399368 | tf_op jit(solution)/shard_map/ppermute | solution.py:19
  5.8 8.1 %collective-permute-start.1 = (f32[65,1,512]{2,1,0:T(1,128)S(1)}, f32[65,1,512]{2,1,0:T(1,128)S(1)}, u32[]{:S(2)}, u32[]{:S(2)}) collective-permute-start(f32[65,1,512]{2,1,0:T(1,128)S(1)} %get-tuple-element.432), channel_id=1, source_target_pairs={{1,0},{2,1},{3,2},{4,3},{5,4},{6,5},{7,6},{8,7},{9,8},{10,9},{11,1... | collective-permute-start | bytes 399368 | tf_op jit(solution)/shard_map/ppermute | solution.py:22
  14.3 0.2 reduce_window_sum.11
  14.5 0.2 select_reduce_fusion
  14.9 0.3 fusion.18
  15.2 0.7 all_to_all.9
  15.9 6.0 %all-to-all-start = ((f32[128,1,8]{2,1,0:T(1,128)}), f32[128,1,8]{2,1,0:T(1,128)S(1)}, u32[]{:S(2)}, u32[]{:S(2)}) async-start(f32[128,1,8]{2,1,0:T(1,128)} %bitcast.4), calls=%async_computation | async-start | bytes 131072 | tf_op jit(solution)/shard_map/all_to_all | solution.py:117
  22.0 0.2 broadcast_compare_fusion
  22.3 0.7 fusion.30
  23.0 2.8 %convolution_bitcast_fusion = f32[32,4,4,128]{3,2,1,0:T(4,128)S(1)} fusion(bf16[32,4,128,128]{3,2,1,0:T(8,128)(2,1)} %param.20, bf16[4,32,128]{2,1,0:T(8,128)(2,1)S(1)} %reshape.185), kind=kOutput, calls=%fused_computation | convolution fusion | flops 16777216 | bytes 4489216 | tf_op jit(solution)/shard_map/bfi,bkij->bkfj/dot_general | solution.py:101
  25.8 0.1 reshape.193
  26.0 2.4 %fusion.16 = f32[128,8,512]{2,1,0:T(8,128)} fusion(f32[128,512,1]{1,0,2:T(8,128)S(1)} %reshape.193, pred[128,8,128]{2,0,1:T(32,128)(4,1)S(1)} %broadcast_compare_fusion), kind=kOutput, calls=%fused_computation.25 | convolution fusion | flops 805306368 | bytes 2490368 | tf_op jit(solution)/shard_map/dot_general | solution.py:71
  28.4 2.0 %all-to-all-done = f32[128,1,8]{2,1,0:T(1,128)S(1)} async-done(((f32[128,1,8]{2,1,0:T(1,128)}), f32[128,1,8]{2,1,0:T(1,128)S(1)}, u32[]{:S(2)}, u32[]{:S(2)}) %all-to-all-start) | async-done | bytes 4128 | tf_op jit(solution)/shard_map/all_to_all | solution.py:117
  30.4 0.6 copy-done.191
  31.0 8.2 %all-to-all-start.1 = ((f32[128,8,512]{2,1,0:T(8,128)}), f32[128,8,512]{2,1,0:T(8,128)}, u32[]{:S(2)}, u32[]{:S(2)}) async-start(f32[128,8,512]{2,1,0:T(8,128)} %fusion.16), calls=%async_computation.1 | async-start | bytes 4194304 | tf_op jit(solution)/shard_map/all_to_all | solution.py:110
  39.3 0.7 pad.28
  40.0 0.6 pad.30
  40.6 0.5 iota_convert_fusion
  41.2 0.7 negate_divide_fusion.55
  41.9 0.8 fusion.206
  42.7 1.7 %fusion.443 = (f32[64,8,511]{2,1,0:T(8,128)}, f32[64,8,511]{2,1,0:T(8,128)}) fusion(f32[64,8,512]{2,1,0:T(8,128)S(1)} %copy-done), kind=kLoop, calls=%fused_computation.1356 | loop fusion | bytes 4186112 | tf_op jit(solution)/shard_map/slice | solution.py:50
  44.5 0.5 broadcast.5799
  44.9 0.7 reduce.8
  45.8 2.4 %fusion.12 = f32[64,8,512]{2,1,0:T(8,128)S(1)} fusion(f32[64,8,512]{2,1,0:T(8,128)S(1)} %copy-done, f32[65,1,512]{2,1,0:T(1,128)S(1)} %collective-permute-done.1, f32[1,8,512]{2,1,0:T(8,128)S(1)} %bitcast.3017, f32[65,1,512]{2,1,0:T(1,128)S(1)} %collective-permute-done, f32[64,8,511]{2,1,0:T(8,128)} %get-tuple-element.437, ...), kind=kLoop, calls=%fused_computation.17 | loop fusion | flops 4456448 | bytes 4554752 | tf_op jit(solution)/shard_map/add | solution.py:60
  48.2 20.3 %all-to-all-done.1 = f32[128,8,512]{2,1,0:T(8,128)} async-done(((f32[128,8,512]{2,1,0:T(8,128)}), f32[128,8,512]{2,1,0:T(8,128)}, u32[]{:S(2)}, u32[]{:S(2)}) %all-to-all-start.1) | async-done | bytes 2097184 | tf_op jit(solution)/shard_map/all_to_all | solution.py:110
  68.5 3.0 %copy.25 = f32[512,1024]{1,0:T(8,128)} copy(f32[512,1024]{0,1:T(8,128)} %bitcast.12) | data formatting | bytes 4194304 | tf_op jit(solution)/shard_map/dot_general | solution.py:127
  71.7 3.4 %fusion.445 = (f32[32,128]{1,0:T(8,128)S(1)}, f32[4,32,128]{2,1,0:T(8,128)}) fusion(f32[4,128,1024]{2,1,0:T(8,128)} %bitcast.3014, f32[1024]{0:T(1024)S(1)} %eq.68, f32[32]{0:T(128)S(1)} %copy-done.211), kind=kOutput, calls=%fused_computation.1358 | convolution fusion | flops 201371648 | bytes 2183296 | tf_op jit(solution)/shard_map/dot_general | solution.py:127
  75.4 0.1 fusion.214
  75.6 1.0 fusion.100
  77.0 1.1 constant_dynamic-update-slice_fusion.128
  78.4 1.0 add_divide_fusion.41
  79.9 1.2 %constant_dynamic-update-slice_fusion.127 = (f32[65,8,512]{2,1,0:T(8,128)S(1)}, f32[1,8,512]{2,1,0:T(8,128)S(1)}, f32[1,8,512]{2,1,0:T(8,128)S(1)}, f32[1,8,512]...) fusion(f32[65,8,512]{2,1,0:T(8,128)S(1)} %get-tuple-element.185, ...), kind=kLoop, calls=%fused_computation.156 | loop fusion | flops 1490944 | bytes 3096576
  82.2 1.0 copy-done.1
  83.2 0.9 fusion.441
  84.1 1.9 %collective-permute-start.2 = (f32[65,1,512]{2,1,0:T(1,128)}, f32[65,1,512]{2,1,0:T(1,128)S(1)}, u32[]{:S(2)}, u32[]{:S(2)}) collective-permute-start(f32[65,1,512]{2,1,0:T(1,128)} %get-tuple-element.427), channel_id=1, source_target_pairs={{0,1},{1,2},{2,3},{3,4},{4,5},{5,6},{6,7},{7,8},{8,9},{9,10},{10,1... | collective-permute-start | bytes 399368 | tf_op jit(solution)/shard_map/ppermute | solution.py:19
  86.0 8.0 %collective-permute-start.3 = (f32[65,1,512]{2,1,0:T(1,128)}, f32[65,1,512]{2,1,0:T(1,128)S(1)}, u32[]{:S(2)}, u32[]{:S(2)}) collective-permute-start(f32[65,1,512]{2,1,0:T(1,128)} %get-tuple-element.428), channel_id=1, source_target_pairs={{1,0},{2,1},{3,2},{4,3},{5,4},{6,5},{7,6},{8,7},{9,8},{10,9},{11,1... | collective-permute-start | bytes 399368 | tf_op jit(solution)/shard_map/ppermute | solution.py:22
  94.1 1.7 %fusion.442 = (f32[64,8,511]{2,1,0:T(8,128)}, f32[64,8,511]{2,1,0:T(8,128)}) fusion(f32[64,8,512]{2,1,0:T(8,128)S(1)} %get-tuple-element.439), kind=kLoop, calls=%fused_computation.1355 | loop fusion | bytes 4186112 | tf_op jit(solution)/shard_map/slice | solution.py:50
  95.8 1.5 %reshape.189 = f32[4,8,512]{2,1,0:T(8,128)} reshape(f32[4,32,128]{2,1,0:T(8,128)} %get-tuple-element.565) | data formatting | bytes 131072 | tf_op jit(solution)/shard_map/reshape | solution.py:128
  97.4 1.1 copy-done.3
  98.5 2.1 %fusion.4 = f32[64,8,512]{2,1,0:T(8,128)S(1)} fusion(f32[64,8,512]{2,1,0:T(8,128)S(1)} %get-tuple-element.439, f32[65,1,512]{2,1,0:T(1,128)S(1)} %collective-permute-done.3, f32[65,8,512]{2,1,0:T(8,128)S(1)} %copy-done.2, f32[65,1,512]{2,1,0:T(1,128)S(1)} %collective-permute-done.2, f32[64,8,511]{2,1,0:T(8,128)} %get-tuple-element.434, ...), kind=kLoop, calls=%fused_computation.7 | loop fusion | flops 3932160 | bytes 5603328 | tf_op jit(solution)/shard_map/add | solution.py:60
  101.1 1.5 %add_divide_fusion.1 = (f32[1,8,512]{2,1,0:T(8,128)S(1)}, f32[1,8,512]{2,1,0:T(8,128)S(1)}, f32[1,8,512]{2,1,0:T(8,128)S(1)}, f32[1,8,512]{2,1,0:T(8,128)S(1)}, ...) fusion(f32[1,8,512]{2,1,0:T(8,128)} %copy-done.100, ...), kind=kLoop, calls=%fused_computation.1047 | loop fusion | flops 532480 | bytes 2670592 | tf_op jit(solution)/shard_map/eval_jaxpr/div | solution.py:34
  103.0 1.4 %fusion.34 = (f32[8,512]{1,0:T(8,128)S(1)}, f32[8,512]{1,0:T(8,128)S(1)}, f32[8,512]{1,0:T(8,128)S(1)}, f32[8,512]{1,0:T(8,128)S(1)}, f32[8,512]{1,0:T(8,128)S(1...) fusion(f32[8,512]{1,0:T(8,128)S(1)} %copy-done.55, ...), kind=kLoop, calls=%fused_computation.252 | loop fusion | flops 757760 | bytes 3670016 | tf_op jit(solution)/shard_map/eval_jaxpr/div | solution.py:34
  104.8 1.4 %constant_dynamic-update-slice_fusion.192 = (f32[64,8,512]{2,1,0:T(8,128)S(1)}, f32[8,512]{1,0:T(8,128)S(1)}, f32[8,512]{1,0:T(8,128)S(1)}, f32[8,512]{1,0:T(8,1...) fusion(f32[8,512]{1,0:T(8,128)S(1)} %get-tuple-element.141, ...), kind=kLoop, calls=%fused_computation.221 | loop fusion | flops 1265663 | bytes 3162112
  106.6 1.3 %constant_dynamic-update-slice_fusion.191 = (f32[64,8,512]{2,1,0:T(8,128)S(1)}, f32[1,8,512]{2,1,0:T(8,128)S(1)}, f32[1,8,512]{2,1,0:T(8,128)S(1)}, f32[1,8,512]...) fusion(f32[64,8,512]{2,1,0:T(8,128)S(1)} %get-tuple-element.90,, ...), kind=kLoop, calls=%fused_computation.220 | loop fusion | flops 1495040 | bytes 2785280
  108.6 0.1 copy-done.199
  109.1 1.0 copy-done.212
  (571 shorter events, 2.5 us)
Async XLA Ops:
  0.6 13.3 %copy-start.208 = (s32[32,4]{0,1:T(4,128)S(1)}, s32[32,4]{0,1:T(4,128)}, u32[]{:S(2)}) copy-start(s32[32,4]{0,1:T(4,128)} %param.21) | copy-start | bytes 1540
  0.6 13.3 %copy-start.209 = (s32[32,4]{0,1:T(4,128)S(1)}, s32[32,4]{0,1:T(4,128)}, u32[]{:S(2)}) copy-start(s32[32,4]{0,1:T(4,128)} %param.23) | copy-start | bytes 1540
  0.7 14.0 %copy-start.210 = (s32[32,4]{0,1:T(4,128)S(1)}, s32[32,4]{0,1:T(4,128)}, u32[]{:S(2)}) copy-start(s32[32,4]{0,1:T(4,128)} %param.22) | copy-start | bytes 1540
  2.0 20.2 %copy-start = (f32[64,8,512]{2,1,0:T(8,128)S(1)}, f32[64,8,512]{2,1,0:T(8,128)}, u32[]{:S(2)}) copy-start(f32[64,8,512]{2,1,0:T(8,128)} %param.14) | copy-start | bytes 3145732
  3.9 18.3 %collective-permute-start = (f32[65,1,512]{2,1,0:T(1,128)S(1)}, f32[65,1,512]{2,1,0:T(1,128)S(1)}, u32[]{:S(2)}, u32[]{:S(2)}) collective-permute-start(f32[65,1,512]{2,1,0:T(1,128)S(1)} %get-tuple-element.431), channel_id=1, source_target_pairs={{0,1},{1,2},{2,3},{3,4},{4,5},{5,6},{6,7},{7,8},{8,9},{9,10},{10,1... | collective-permute-start | bytes 399368 | tf_op jit(solution)/shard_map/ppermute | solution.py:19
  5.8 16.4 %collective-permute-start.1 = (f32[65,1,512]{2,1,0:T(1,128)S(1)}, f32[65,1,512]{2,1,0:T(1,128)S(1)}, u32[]{:S(2)}, u32[]{:S(2)}) collective-permute-start(f32[65,1,512]{2,1,0:T(1,128)S(1)} %get-tuple-element.432), channel_id=1, source_target_pairs={{1,0},{2,1},{3,2},{4,3},{5,4},{6,5},{7,6},{8,7},{9,8},{10,9},{11,1... | collective-permute-start | bytes 399368 | tf_op jit(solution)/shard_map/ppermute | solution.py:22
  14.3 8.7 %copy-start.204 = (f32[4,8,512]{2,1,0:T(8,128)S(1)}, f32[4,8,512]{2,1,0:T(8,128)}, u32[]{:S(2)}) copy-start(f32[4,8,512]{2,1,0:T(8,128)} %param.18) | copy-start | bytes 196612
  14.3 8.7 %copy-start.205 = (f32[4,8,512]{2,1,0:T(8,128)S(1)}, f32[4,8,512]{2,1,0:T(8,128)}, u32[]{:S(2)}) copy-start(f32[4,8,512]{2,1,0:T(8,128)} %param.19) | copy-start | bytes 196612
  15.9 14.4 %all-to-all-start = ((f32[128,1,8]{2,1,0:T(1,128)}), f32[128,1,8]{2,1,0:T(1,128)S(1)}, u32[]{:S(2)}, u32[]{:S(2)}) async-start(f32[128,1,8]{2,1,0:T(1,128)} %bitcast.4), calls=%async_computation | async-start | bytes 131072 | tf_op jit(solution)/shard_map/all_to_all | solution.py:117
  22.2 3.6 %copy-start.206 = (f32[8]{0:T(128)}, f32[8]{0:T(128)S(1)}, u32[]{:S(2)}) copy-start(f32[8]{0:T(128)S(1)} %get-tuple-element.567) | copy-start | bytes 100
  28.4 12.7 %copy-start.4 = (f32[63,8,512]{2,1,0:T(8,128)S(1)}, f32[63,8,512]{2,1,0:T(8,128)}, u32[]{:S(2)}) copy-start(f32[63,8,512]{2,1,0:T(8,128)} %param.15) | copy-start | bytes 3096580
  31.0 37.5 %all-to-all-start.1 = ((f32[128,8,512]{2,1,0:T(8,128)}), f32[128,8,512]{2,1,0:T(8,128)}, u32[]{:S(2)}, u32[]{:S(2)}) async-start(f32[128,8,512]{2,1,0:T(8,128)} %fusion.16), calls=%async_computation.1 | async-start | bytes 4194304 | tf_op jit(solution)/shard_map/all_to_all | solution.py:110
  42.7 34.3 %copy-start.5 = (f32[8,512]{1,0:T(8,128)}, f32[8,512]{1,0:T(8,128)S(1)}, u32[]{:S(2)}) copy-start(f32[8,512]{1,0:T(8,128)S(1)} %get-tuple-element.392) | copy-start | bytes 49156
  42.7 2.2 %copy-start.192 = (f32[128,1,8]{2,1,0:T(1,128)S(1)}, f32[128,1,8]{2,1,0:T(1,128)}, u32[]{:S(2)}) copy-start(f32[128,1,8]{2,1,0:T(1,128)} %copy-done.191) | copy-start | bytes 12292
  68.5 3.0 %copy-start.211 = (f32[32]{0:T(128)S(1)}, f32[32]{0:T(128)}, u32[]{:S(2)}) copy-start(f32[32]{0:T(128)} %iota_convert_fusion) | copy-start | bytes 388
  71.5 3.7 %copy-start.43 = (f32[1,8,512]{2,1,0:T(8,128)S(1)}, f32[1,8,512]{2,1,0:T(8,128)}, u32[]{:S(2)}) copy-start(f32[1,8,512]{2,1,0:T(8,128)} %get-tuple-element.295) | copy-start | bytes 49156
  71.5 3.7 %copy-start.46 = (f32[1,8,512]{2,1,0:T(8,128)S(1)}, f32[1,8,512]{2,1,0:T(8,128)}, u32[]{:S(2)}) copy-start(f32[1,8,512]{2,1,0:T(8,128)} %get-tuple-element.298) | copy-start | bytes 49156
  71.5 3.7 %copy-start.49 = (f32[1,8,512]{2,1,0:T(8,128)S(1)}, f32[1,8,512]{2,1,0:T(8,128)}, u32[]{:S(2)}) copy-start(f32[1,8,512]{2,1,0:T(8,128)} %get-tuple-element.301) | copy-start | bytes 49156
  71.5 3.7 %copy-start.200 = (f32[1,8,512]{2,1,0:T(8,128)S(1)}, f32[1,8,512]{2,1,0:T(8,128)}, u32[]{:S(2)}) copy-start(f32[1,8,512]{2,1,0:T(8,128)} %get-tuple-element.294) | copy-start | bytes 49156
  71.5 3.7 %copy-start.201 = (f32[1,8,512]{2,1,0:T(8,128)S(1)}, f32[1,8,512]{2,1,0:T(8,128)}, u32[]{:S(2)}) copy-start(f32[1,8,512]{2,1,0:T(8,128)} %get-tuple-element.297) | copy-start | bytes 49156
  71.5 3.7 %copy-start.202 = (f32[1,8,512]{2,1,0:T(8,128)S(1)}, f32[1,8,512]{2,1,0:T(8,128)}, u32[]{:S(2)}) copy-start(f32[1,8,512]{2,1,0:T(8,128)} %get-tuple-element.300) | copy-start | bytes 49156
  71.5 3.7 %copy-start.7 = (f32[8,512]{1,0:T(8,128)S(1)}, f32[8,512]{1,0:T(8,128)}, u32[]{:S(2)}) copy-start(f32[8,512]{1,0:T(8,128)} %get-tuple-element.393) | copy-start | bytes 49156
  71.5 3.7 %copy-start.9 = (f32[8,512]{1,0:T(8,128)S(1)}, f32[8,512]{1,0:T(8,128)}, u32[]{:S(2)}) copy-start(f32[8,512]{1,0:T(8,128)} %get-tuple-element.394) | copy-start | bytes 49156
  71.5 3.7 %copy-start.11 = (f32[8,512]{1,0:T(8,128)S(1)}, f32[8,512]{1,0:T(8,128)}, u32[]{:S(2)}) copy-start(f32[8,512]{1,0:T(8,128)} %get-tuple-element.395) | copy-start | bytes 49156
  71.5 3.7 %copy-start.13 = (f32[8,512]{1,0:T(8,128)S(1)}, f32[8,512]{1,0:T(8,128)}, u32[]{:S(2)}) copy-start(f32[8,512]{1,0:T(8,128)} %get-tuple-element.396) | copy-start | bytes 49156
  71.5 3.7 %copy-start.15 = (f32[8,512]{1,0:T(8,128)S(1)}, f32[8,512]{1,0:T(8,128)}, u32[]{:S(2)}) copy-start(f32[8,512]{1,0:T(8,128)} %get-tuple-element.397) | copy-start | bytes 49156
  71.6 3.7 %copy-start.17 = (f32[8,512]{1,0:T(8,128)S(1)}, f32[8,512]{1,0:T(8,128)}, u32[]{:S(2)}) copy-start(f32[8,512]{1,0:T(8,128)} %get-tuple-element.398) | copy-start | bytes 49156
  71.6 3.7 %copy-start.19 = (f32[8,512]{1,0:T(8,128)S(1)}, f32[8,512]{1,0:T(8,128)}, u32[]{:S(2)}) copy-start(f32[8,512]{1,0:T(8,128)} %get-tuple-element.399) | copy-start | bytes 49156
  71.6 3.7 %copy-start.21 = (f32[8,512]{1,0:T(8,128)S(1)}, f32[8,512]{1,0:T(8,128)}, u32[]{:S(2)}) copy-start(f32[8,512]{1,0:T(8,128)} %get-tuple-element.400) | copy-start | bytes 49156
  71.6 3.7 %copy-start.23 = (f32[8,512]{1,0:T(8,128)S(1)}, f32[8,512]{1,0:T(8,128)}, u32[]{:S(2)}) copy-start(f32[8,512]{1,0:T(8,128)} %get-tuple-element.401) | copy-start | bytes 49156
  71.6 3.7 %copy-start.25 = (f32[8,512]{1,0:T(8,128)S(1)}, f32[8,512]{1,0:T(8,128)}, u32[]{:S(2)}) copy-start(f32[8,512]{1,0:T(8,128)} %get-tuple-element.402) | copy-start | bytes 49156
  71.6 3.7 %copy-start.27 = (f32[8,512]{1,0:T(8,128)S(1)}, f32[8,512]{1,0:T(8,128)}, u32[]{:S(2)}) copy-start(f32[8,512]{1,0:T(8,128)} %get-tuple-element.403) | copy-start | bytes 49156
  71.6 3.7 %copy-start.29 = (f32[8,512]{1,0:T(8,128)S(1)}, f32[8,512]{1,0:T(8,128)}, u32[]{:S(2)}) copy-start(f32[8,512]{1,0:T(8,128)} %get-tuple-element.404) | copy-start | bytes 49156
  71.6 3.7 %copy-start.31 = (f32[8,512]{1,0:T(8,128)S(1)}, f32[8,512]{1,0:T(8,128)}, u32[]{:S(2)}) copy-start(f32[8,512]{1,0:T(8,128)} %get-tuple-element.405) | copy-start | bytes 49156
  71.6 3.7 %copy-start.33 = (f32[8,512]{1,0:T(8,128)S(1)}, f32[8,512]{1,0:T(8,128)}, u32[]{:S(2)}) copy-start(f32[8,512]{1,0:T(8,128)} %get-tuple-element.406) | copy-start | bytes 49156
  71.6 3.7 %copy-start.35 = (f32[8,512]{1,0:T(8,128)S(1)}, f32[8,512]{1,0:T(8,128)}, u32[]{:S(2)}) copy-start(f32[8,512]{1,0:T(8,128)} %get-tuple-element.407) | copy-start | bytes 49156
  71.7 3.7 %copy-start.37 = (f32[8,512]{1,0:T(8,128)S(1)}, f32[8,512]{1,0:T(8,128)}, u32[]{:S(2)}) copy-start(f32[8,512]{1,0:T(8,128)} %get-tuple-element.408) | copy-start | bytes 49156
  71.7 3.7 %copy-start.39 = (f32[8,512]{1,0:T(8,128)S(1)}, f32[8,512]{1,0:T(8,128)}, u32[]{:S(2)}) copy-start(f32[8,512]{1,0:T(8,128)} %get-tuple-element.409) | copy-start | bytes 49156
  71.7 3.7 %copy-start.41 = (f32[8,512]{1,0:T(8,128)S(1)}, f32[8,512]{1,0:T(8,128)}, u32[]{:S(2)}) copy-start(f32[8,512]{1,0:T(8,128)} %get-tuple-element.410) | copy-start | bytes 49156
  84.1 13.2 %collective-permute-start.2 = (f32[65,1,512]{2,1,0:T(1,128)}, f32[65,1,512]{2,1,0:T(1,128)S(1)}, u32[]{:S(2)}, u32[]{:S(2)}) collective-permute-start(f32[65,1,512]{2,1,0:T(1,128)} %get-tuple-element.427), channel_id=1, source_target_pairs={{0,1},{1,2},{2,3},{3,4},{4,5},{5,6},{6,7},{7,8},{8,9},{9,10},{10,1... | collective-permute-start | bytes 399368 | tf_op jit(solution)/shard_map/ppermute | solution.py:19
  86.0 11.3 %collective-permute-start.3 = (f32[65,1,512]{2,1,0:T(1,128)}, f32[65,1,512]{2,1,0:T(1,128)S(1)}, u32[]{:S(2)}, u32[]{:S(2)}) collective-permute-start(f32[65,1,512]{2,1,0:T(1,128)} %get-tuple-element.428), channel_id=1, source_target_pairs={{1,0},{2,1},{3,2},{4,3},{5,4},{6,5},{7,6},{8,7},{9,8},{10,9},{11,1... | collective-permute-start | bytes 399368 | tf_op jit(solution)/shard_map/ppermute | solution.py:22
  94.1 3.3 %copy-start.2 = (f32[65,8,512]{2,1,0:T(8,128)S(1)}, f32[65,8,512]{2,1,0:T(8,128)}, u32[]{:S(2)}) copy-start(f32[65,8,512]{2,1,0:T(8,128)} %copy-done.1) | copy-start | bytes 3194884
  94.1 3.3 %copy-start.207 = (f32[8]{0:T(128)S(1)}, f32[8]{0:T(128)}, u32[]{:S(2)}) copy-start(f32[8]{0:T(128)} %copy-done.206) | copy-start | bytes 100
  98.5 2.2 %copy-start.45 = (f32[1,8,512]{2,1,0:T(8,128)S(1)}, f32[1,8,512]{2,1,0:T(8,128)}, u32[]{:S(2)}) copy-start(f32[1,8,512]{2,1,0:T(8,128)} %get-tuple-element.295) | copy-start | bytes 49156
  98.5 2.2 %copy-start.48 = (f32[1,8,512]{2,1,0:T(8,128)S(1)}, f32[1,8,512]{2,1,0:T(8,128)}, u32[]{:S(2)}) copy-start(f32[1,8,512]{2,1,0:T(8,128)} %get-tuple-element.298) | copy-start | bytes 49156
  98.5 2.2 %copy-start.51 = (f32[1,8,512]{2,1,0:T(8,128)S(1)}, f32[1,8,512]{2,1,0:T(8,128)}, u32[]{:S(2)}) copy-start(f32[1,8,512]{2,1,0:T(8,128)} %get-tuple-element.301) | copy-start | bytes 49156
  100.7 1.9 %copy-start.6 = (f32[8,512]{1,0:T(8,128)S(1)}, f32[8,512]{1,0:T(8,128)}, u32[]{:S(2)}) copy-start(f32[8,512]{1,0:T(8,128)} %copy-done.5) | copy-start | bytes 49156
  100.7 1.9 %copy-start.8 = (f32[8,512]{1,0:T(8,128)S(1)}, f32[8,512]{1,0:T(8,128)}, u32[]{:S(2)}) copy-start(f32[8,512]{1,0:T(8,128)} %get-tuple-element.393) | copy-start | bytes 49156
  (171 other events, 267.5 us)
where the time goes:
time: 112 us; the launch traced here: 110 us
  starting transfers between devices  34.2 us (31%)
  other arithmetic  22.5 us (20%)
  waiting for transfers between devices  22.3 us (20%)
  local copies, waits for them, and re-layouts  17.1 us (15%)
  matrix products  9.03 us (8%)
  between operations  4.91 us (4%)
    all_to_all x1, waiting for transfers between devices, local(): lax.all_to_all(packed.reshape(groups * tiles, slots, F * 128), ('grp', 't...  20.3 us
    ppermute x2, starting transfers between devices, padded_2(): lax.ppermute(lax.slice_in_dim(block, 0, width, axis=dim), axis, backward)  16.1 us
    all_to_all x1, starting transfers between devices, local(): lax.all_to_all(packed.reshape(groups * tiles, slots, F * 128), ('grp', 't...  8.21 us
    all_to_all x1, starting transfers between devices, local(): lax.all_to_all(tags.reshape(groups * tiles, slots), ('grp', 'tile'), spli...  6.01 us
    unnamed x35, other arithmetic  5.21 us
    div x6, other arithmetic, forward(): r_now = (rhs + low * r_prev) / denom  5.19 us
    unnamed x520, local copies, waits for them, and re-layouts  5.13 us
    add x2, other arithmetic, horizontal(): return field + nu * wet * total  4.57 us
  transfers between devices with their start and end apart: 6, of which 2 were waited for; matrix products, arithmetic and copies ran while one was open for 18% of the time, Pallas kernels for 0%

commit v1 on v0

v1 whole, which is shorter than its diff:
```python
import functools

import jax
import jax.numpy as jnp
from jax import lax
from jax.experimental import pallas as pl
from jax.experimental.pallas import tpu as pltpu
from jax.sharding import PartitionSpec as P

MESH = pl.DeviceIdType.MESH
F32 = jnp.float32
BF16 = jnp.bfloat16
F = 4
K = 4
LEV = 64
HALF = LEV // 2
TILES = 32
SLOTS = 8
MSG = 40
CB = 4
WCH = 8
GAIN = 0.25


def iota(shape, dim):
    return lax.broadcasted_iota(jnp.int32, shape, dim)


def one_hot(mask):
    return jnp.where(mask, 1.0, 0.0).astype(BF16)


def split(x):
    hi = x.astype(BF16)
    return hi, (x - hi.astype(F32)).astype(BF16)


def kernel(
    state_h, vert_h, nu_h, mask_h, coup_h, surf_h, w_h, dt_h, db_h, dg_h,
    out_h, rec_h,
    w_v, st, ve, nu, mask, coup, surf, dt, db, dg,
    xs, terms, slab, got, ps, xr, es, xe,
    se, re, su, ru, coef, wet, inv, ww, mid, rg, ru_fwd, uu, gg, outv, rv,
    lsem, wsem, ssem, rsem, hs, hr, xss, xrs, ess, ers,
):
    grp = lax.axis_index("grp")
    tile = lax.axis_index("tile")
    dev = grp * TILES + tile
    ocean = grp == 3
    n_dev = 4 * TILES

    def dev_id(flat):
        return (flat // TILES, flat % TILES)

    above_dev = dev_id((dev + n_dev - 1) % n_dev)
    below_dev = dev_id((dev + 1) % n_dev)
    t_prev, t_next = (tile + TILES - 1) % TILES, (tile + 1) % TILES

    def load(src, dst, i):
        return pltpu.make_async_copy(src, dst, lsem.at[i])

    small = [
        load(dt_h, dt, 0), load(db_h, db, 1), load(dg_h, dg, 2),
        load(mask_h, mask, 3), load(coup_h, coup, 4), load(surf_h, surf, 5), load(nu_h, nu, 6),
    ]
    st_load = [load(state_h.at[:, :, c * 128:(c + 1) * 128], st.at[c], 7 + c) for c in range(CB)]
    ve_load = [
        load(vert_h.at[:, :, c * 128:(c + 1) * 128], ve.at[c], 11 + c) for c in range(CB)
    ]
    per = 32 // WCH
    w_load = [
        pltpu.make_async_copy(w_h.at[pl.ds(i * per, per)], w_v.at[pl.ds(i * per, per)], wsem.at[i])
        for i in range(WCH)
    ]
    for d in small + st_load + w_load + ve_load:
        d.start()

    barrier = pltpu.get_barrier_semaphore()

    def tell(device):
        pl.semaphore_signal(barrier, inc=1, device_id=device, device_id_type=MESH)

    @pl.loop(1, TILES)
    def _(d):
        tell((grp, (tile + d) % TILES))

    tell(above_dev)
    tell(below_dev)

    @pl.when(ocean)
    def _():
        for g in range(3):
            for t in (tile, t_prev, t_next):
                tell((g, t))

    @pl.when(jnp.logical_not(ocean))
    def _():
        for t in (tile, t_prev, t_next):
            tell((3, t))

    for d in small:
        d.wait()

    lane = iota((1, 128), 1)
    k_of = lane % 4
    b_of = 2 * ((lane % 64) // 4) + lane // 64
    group_label = jnp.where(ocean, 32, 0)
    code = dt[...] * 128 + db[...] + dg[...] * group_label + 1
    code = code.astype(F32)
    wide = jnp.zeros((32, 128), F32)
    for k in range(K):
        wide = jnp.where(k_of == k, code[:, k:k + 1], wide)
    code_row = jnp.sum(jnp.where(iota((32, 128), 0) == b_of, wide, 0.0), axis=0, keepdims=True)
    code_int = code_row.astype(jnp.int32)
    drel = ((code_int // 128) + TILES - tile) % TILES
    label = (code_int % 128).astype(F32)
    i0, i1 = iota((128, 128), 0), iota((128, 128), 1)
    d_row = drel.astype(F32)
    d_col = jnp.sum(jnp.where(i0 == i1, d_row, 0.0), axis=1, keepdims=True)
    pos = jnp.sum(jnp.where((d_col == d_row) & (i0 < i1), 1.0, 0.0), axis=0, keepdims=True)
    slot = drel * SLOTS + pos.astype(jnp.int32)
    tag_a = jnp.where(iota((TILES, 128), 0) == drel, label, 0.0).astype(BF16)
    tag_b = one_hot(i0 == slot % 128)
    tags = lax.dot_general(tag_a, tag_b, (((1,), (1,)), ((), ())), preferred_element_type=F32)
    for j in range(TILES // 8):
        slab[pl.ds(j * 8 * MSG + 32, 8, stride=MSG), :] = tags[j * 8:(j + 1) * 8]

    for d in st_load:
        d.wait()
    for c in range(CB):
        cs = slice(c * 128, (c + 1) * 128)
        wet_c = jnp.where(ocean, mask[:, cs].astype(F32), 1.0)
        wet[c] = wet_c
        for f in range(F):
            send = coup[f, :, cs] * (st[c, 0] - surf[f, :, cs]) * wet_c
            xs[pl.ds(c * 4 + f, 8, stride=16), :] = send

    for c in range(CB):
        rows = st.at[c].reshape(LEV * 8, 128)
        for side in range(2):
            se[side, c, 0:LEV, :] = rows[pl.ds(7 * side, LEV, stride=8), :]
            se[side, c, LEV:LEV + 8, :] = wet[c]

    @pl.when(ocean)
    def _():
        pl.semaphore_wait(barrier, 31 + 2 + 9)

    @pl.when(jnp.logical_not(ocean))
    def _():
        pl.semaphore_wait(barrier, 31 + 2 + 3)

    def halo(src, dst, side, i):
        return pltpu.make_async_remote_copy(
            src_ref=src.at[side], dst_ref=dst.at[side], send_sem=hs.at[i, side],
            recv_sem=hr.at[i, side], device_id=above_dev if side == 0 else below_dev,
            device_id_type=MESH,
        )

    edge = [halo(se, re, side, 0) for side in range(2)]
    for d in edge:
        d.start()

    row8 = iota((8, 128), 0)

    def two_blocks(q):
        x8 = xs[pl.ds(q * 8, 8), :]
        x = jnp.concatenate(
            [jnp.where(row8 < 4, x8, 0.0), jnp.where(row8 < 4, 0.0, x8)], axis=1
        ).astype(BF16)
        for kp in range(2):
            cols = [w_v[pl.ds(2 * q, 2), 2 * kp + j].reshape(256, 128) for j in range(2)]
            t = jnp.dot(x, jnp.concatenate(cols, axis=1), preferred_element_type=F32)
            for j in range(2):
                terms[pl.ds(q * 4 + 2 * kp + j, 8, stride=64), :] = t[:, j * 128:(j + 1) * 128]

    for i in range(WCH):
        w_load[i].wait()
        for q in range(i * 16 // WCH, (i + 1) * 16 // WCH):
            two_blocks(q)

    his, los = [], []
    for f in range(F):
        t = jnp.concatenate([terms[bl * 256 + f * 64:bl * 256 + f * 64 + 64, :] for bl in range(2)], 0)
        hi, lo = split(t)
        his.append(hi)
        los.append(lo)
    hi = jnp.concatenate(his, axis=1)
    lo = jnp.concatenate(los, axis=1)

    def a2a(d):
        return pltpu.make_async_remote_copy(
            src_ref=slab.at[pl.ds(d * MSG, MSG)], dst_ref=got.at[pl.ds(d * MSG, MSG)],
            send_sem=ssem.at[d], recv_sem=rsem.at[d],
            device_id=(grp, (tile + d) % TILES), device_id_type=MESH,
        )

    parts = 4
    rows = TILES * SLOTS // parts
    for p in range(parts):
        ch = one_hot(iota((rows, 128), 0) + p * rows == slot)
        packed = jnp.dot(ch, hi, preferred_element_type=F32) + jnp.dot(
            ch, lo, preferred_element_type=F32
        )
        for j in range(TILES // parts):
            d = p * (TILES // parts) + j
            for f in range(F):
                slab[d * MSG + f * 8:d * MSG + f * 8 + 8, :] = packed[
                    j * 8:(j + 1) * 8, f * 128:(f + 1) * 128
                ]

        @pl.loop(max(1, p * (TILES // parts)), (p + 1) * (TILES // parts))
        def _(d):
            a2a(d).start()

    for d in ve_load:
        d.wait()
    inv[0, 0] = jnp.ones((8, 128), F32)
    inv[0, 1] = jnp.zeros((8, 128), F32)
    one, zero = inv[0, 0], inv[0, 1]
    wets = [wet[c] for c in range(CB)]

    def factor(i, carry):
        e_t, e_b, _, r_g = carry
        n_t, n_b, n_g = [], [], []
        for c in range(CB):
            a_t = ve[c, i] * wets[c]
            a_b = ve[c, LEV - 2 - i] * wets[c]
            i_t = 1.0 / (e_t[c] + a_t)
            i_b = 1.0 / (e_b[c] + a_b)
            w_t, w_b = a_t * i_t, a_b * i_b
            inv[c, i] = i_t
            inv[c, LEV - 1 - i] = i_b
            ww[c, i] = w_t
            ww[c, LEV - 1 - i] = w_b
            rg[c, i] = r_g[c]
            n_t.append(1.0 + w_t * e_t[c])
            n_b.append(1.0 + w_b * e_b[c])
            n_g.append(w_t * r_g[c])
        return n_t, n_b, e_b, n_g

    ones = [one] * CB
    zeros = [zero] * CB
    e_t, _, e_b, r_g = lax.fori_loop(0, HALF, factor, (ones, ones, ones, ones), unroll=2)
    mids = [1.0 / (e_t[c] + e_b[c] - 1.0) for c in range(CB)]
    for c in range(CB):
        mid[c] = mids[c]

    for d in edge:
        d.wait_recv()
    lane8 = iota((8, 128), 1)
    keep_above = jnp.where((dev != 0) & (dev != 96), 1.0, 0.0)
    keep_below = jnp.where((dev != 127) & (dev != 95), 1.0, 0.0)

    def neighbours(x, up, dn):
        ls = [pltpu.roll(x[c], 1, 1) for c in range(CB)]
        rs = [pltpu.roll(x[c], 127, 1) for c in range(CB)]
        out = []
        for c in range(CB):
            left = ls[c] if c == 0 else jnp.where(lane8 == 0, ls[c - 1], ls[c])
            right = rs[c] if c == CB - 1 else jnp.where(lane8 == 127, rs[c + 1], rs[c])
            above = jnp.where(row8 == 0, up[c], pltpu.roll(x[c], 1, 0))
            below = jnp.where(row8 == 7, dn[c], pltpu.roll(x[c], 7, 0))
            out.append((left, right, above, below))
        return out

    wet_up = [re[1, c, LEV + 7:LEV + 8, :] for c in range(CB)]
    wet_dn = [re[0, c, LEV:LEV + 1, :] for c in range(CB)]
    around = neighbours(
        wets, [w * keep_above for w in wet_up], [w * keep_below for w in wet_dn]
    )
    for c in range(CB):
        left, right, above, below = around[c]
        if c == 0:
            left = jnp.where(lane8 == 0, 0.0, left)
        if c == CB - 1:
            right = jnp.where(lane8 == 127, 0.0, right)
        scale = nu[:, c * 128:(c + 1) * 128] * wets[c]
        cs = [scale * v for v in (left, right, above, below)]
        for j in range(4):
            coef[j, c] = cs[j]
        coef[4, c] = 1.0 - (cs[0] + cs[1] + cs[2] + cs[3])

    def spread(x, up, dn):
        out = []
        for c, near in enumerate(neighbours(x, up, dn)):
            total = coef[4, c] * x[c]
            for j in range(4):
                total = total + coef[j, c] * near[j]
            out.append(total)
        return out

    def halo_rows(ref, l):
        return [ref[c, pl.ds(l, 1), :] for c in range(CB)]

    def first(i, carry):
        r_t, r_b = carry
        l_t, l_b = i, LEV - 1 - i
        h_t = spread([st[c, l_t] for c in range(CB)], halo_rows(re.at[1], l_t), halo_rows(re.at[0], l_t))
        h_b = spread([st[c, l_b] for c in range(CB)], halo_rows(re.at[1], l_b), halo_rows(re.at[0], l_b))
        n_t, n_b = [], []
        for c in range(CB):
            r = h_t[c] + r_t[c]
            s = h_b[c] + r_b[c]
            ru_fwd[c, l_t] = r
            ru_fwd[c, l_b] = s
            n_t.append(ww[c, l_t] * r)
            n_b.append(ww[c, l_b] * s)
        return n_t, n_b

    r_t, _ = lax.fori_loop(0, HALF, first, (zeros, zeros))
    x_b, x_t, y_b, y_t = [], [], [], []
    for c in range(CB):
        x32 = (ru_fwd[c, HALF] + r_t[c]) * mids[c]
        y32 = r_g[c] * mids[c]
        x_t.append(x32)
        y_t.append(y32)
        x_b.append(inv[c, HALF - 1] * ru_fwd[c, HALF - 1] + ww[c, HALF - 1] * x32)
        y_b.append(inv[c, HALF - 1] * rg[c, HALF - 1] + ww[c, HALF - 1] * y32)

    def back(i, carry):
        x_t, x_b, y_t, y_b = carry
        l_t, l_b = HALF - 1 - i, HALF + i
        n = [[], [], [], []]
        for c in range(CB):
            w_t, w_b, i_t, i_b = ww[c, l_t], ww[c, l_b], inv[c, l_t], inv[c, l_b]
            x0 = i_t * ru_fwd[c, l_t] + w_t * x_t[c]
            x1 = i_b * ru_fwd[c, l_b] + w_b * x_b[c]
            y0 = i_t * rg[c, l_t] + w_t * y_t[c]
            y1 = w_b * y_b[c]
            uu[c, l_t] = x0
            uu[c, l_b] = x1
            gg[c, l_t] = y0
            gg[c, l_b] = y1
            for a, v in zip(n, (x0, x1, y0, y1)):
                a.append(v)
        return tuple(n)

    lax.fori_loop(0, HALF, back, (x_t, x_b, y_t, y_b), unroll=2)

    for c in range(CB):
        rows_u = uu.at[c].reshape(LEV * 8, 128)
        rows_g = gg.at[c].reshape(LEV * 8, 128)
        for side in range(2):
            su[side, 0, c] = rows_u[pl.ds(7 * side, LEV, stride=8), :]
            su[side, 1, c] = rows_g[pl.ds(7 * side, LEV, stride=8), :]
    edge_u = [halo(su, ru, side, 1) for side in range(2)]
    for d in edge_u:
        d.start()

    got[0:MSG, :] = slab[0:MSG, :]

    @pl.loop(1, TILES)
    def _(d):
        a2a(d).wait_recv()

    halves = []
    for h in range(2):
        t = got[pl.ds(h * 16 * MSG + 32, 8, stride=MSG), :] + got[
            pl.ds((h * 16 + 8) * MSG + 32, 8, stride=MSG), :
        ]
        halves.append(jnp.sum(t, axis=0, keepdims=True))
    tag_row = jnp.concatenate(halves, axis=1)
    m = iota((96, 256), 0)
    want = (m // 32) * 32 + (m % 8) * 4 + (m % 32) // 8 + 1
    ch2 = one_hot(want.astype(F32) == tag_row)
    for f in range(F):
        items = jnp.concatenate(
            [got[d * MSG + f * 8:d * MSG + f * 8 + 8, :] for d in range(TILES)], axis=0
        )
        hi, lo = split(items)
        part = jnp.dot(ch2, hi, preferred_element_type=F32) + jnp.dot(
            ch2, lo, preferred_element_type=F32
        )
        for g in range(3):
            for c in range(CB):
                ps[g, c, f] = part[g * 32 + c * 8:g * 32 + c * 8 + 8]
    for g in range(3):
        for c in range(CB):
            tot = ps[g, c, 0] + ps[g, c, 1] + ps[g, c, 2] + ps[g, c, 3]
            es[g, 0, c:c + 1, :] = tot[0:1]
            es[g, 1, c:c + 1, :] = tot[7:8]

    def across(g, src, to, j):
        return pltpu.make_async_remote_copy(
            src_ref=src, dst_ref=xr.at[j], send_sem=xss.at[g], recv_sem=xrs.at[j],
            device_id=to, device_id_type=MESH,
        )

    def across_edge(g, side, to, j):
        return pltpu.make_async_remote_copy(
            src_ref=es.at[g, side], dst_ref=xe.at[j, side], send_sem=ess.at[g, side],
            recv_sem=ers.at[j, side], device_id=to, device_id_type=MESH,
        )

    def ocean_sends():
        copies = []
        for g in range(3):
            copies.append(across_edge(g, 0, dev_id((g * TILES + tile + 95) % 96), 0))
            copies.append(across_edge(g, 1, dev_id((g * TILES + tile + 1) % 96), 0))
            copies.append(across(g, ps.at[g], (g, tile), 0))
        return copies

    def air_sends():
        return [
            across_edge(0, 0, (3, t_prev), grp),
            across_edge(0, 1, (3, t_next), grp),
            across(0, ps.at[0], (3, tile), grp),
        ]

    @pl.when(ocean)
    def _():
        for d in ocean_sends():
            d.start()
        for j in range(3):
            across(j, ps.at[0], (0, tile), j).wait_recv()
            for side in range(2):
                across_edge(j, side, (0, tile), j).wait_recv()

    @pl.when(jnp.logical_not(ocean))
    def _():
        for d in air_sends():
            d.start()
        for j in range(1, 3):
            xr[j] = jnp.zeros(xr.shape[1:], F32)
            xe[j] = jnp.zeros(xe.shape[1:], F32)
        across(0, ps.at[0], (3, tile), 0).wait_recv()
        for side in range(2):
            across_edge(0, side, (3, tile), 0).wait_recv()

    forc, f_up, f_dn = [], [], []
    e_up = (xe[0, 1] + xe[1, 1] + xe[2, 1]) * GAIN
    e_dn = (xe[0, 0] + xe[1, 0] + xe[2, 0]) * GAIN
    for c in range(CB):
        tot = None
        for f in range(F):
            r = xr[0, c, f] + xr[1, c, f] + xr[2, c, f]
            rv[c, f] = r
            tot = r if tot is None else tot + r
        forc.append(GAIN * wets[c] * tot)
        f_up.append(e_up[c:c + 1] * wet_up[c])
        f_dn.append(e_dn[c:c + 1] * wet_dn[c])
    rec_out = [
        pltpu.make_async_copy(rv.at[c], rec_h.at[:, :, c * 128:(c + 1) * 128], lsem.at[c])
        for c in range(CB)
    ]
    for d in rec_out:
        d.start()

    for d in edge_u:
        d.wait_recv()

    def level(l):
        x = [uu[c, l] + gg[c, l] * forc[c] for c in range(CB)]
        up = [
            ru[1, 0, c, pl.ds(l, 1), :] + ru[1, 1, c, pl.ds(l, 1), :] * f_up[c] for c in range(CB)
        ]
        dn = [
            ru[0, 0, c, pl.ds(l, 1), :] + ru[0, 1, c, pl.ds(l, 1), :] * f_dn[c] for c in range(CB)
        ]
        return spread(x, up, dn)

    def second(i, carry):
        r_t, r_b = carry
        l_t, l_b = i, LEV - 1 - i
        h_t, h_b = level(l_t), level(l_b)
        n_t, n_b = [], []
        for c in range(CB):
            r = h_t[c] + r_t[c]
            s = h_b[c] + r_b[c]
            ru_fwd[c, l_t] = r
            ru_fwd[c, l_b] = s
            n_t.append(ww[c, l_t] * r)
            n_b.append(ww[c, l_b] * s)
        return n_t, n_b

    r_t, _ = lax.fori_loop(0, HALF, second, (forc, zeros))
    x_t, x_b = [], []
    for c in range(CB):
        x32 = (ru_fwd[c, HALF] + r_t[c]) * mid[c]
        x_t.append(x32)
        x_b.append(inv[c, HALF - 1] * ru_fwd[c, HALF - 1] + ww[c, HALF - 1] * x32)

    def back2(i, carry):
        x_t, x_b = carry
        l_t, l_b = HALF - 1 - i, HALF + i
        n_t, n_b = [], []
        for c in range(CB):
            x0 = inv[c, l_t] * ru_fwd[c, l_t] + ww[c, l_t] * x_t[c]
            x1 = inv[c, l_b] * ru_fwd[c, l_b] + ww[c, l_b] * x_b[c]
            outv[c, l_t] = x0
            outv[c, l_b] = x1
            n_t.append(x0)
            n_b.append(x1)
        return n_t, n_b

    lax.fori_loop(0, HALF, back2, (x_t, x_b), unroll=2)
    st_out = [
        pltpu.make_async_copy(outv.at[c], out_h.at[:, :, c * 128:(c + 1) * 128], lsem.at[4 + c])
        for c in range(CB)
    ]
    for d in st_out:
        d.start()

    for d in edge + edge_u:
        d.wait_send()

    @pl.loop(1, TILES)
    def _(d):
        a2a(d).wait_send()

    @pl.when(ocean)
    def _():
        for d in ocean_sends():
            d.wait_send()

    @pl.when(jnp.logical_not(ocean))
    def _():
        for d in air_sends():
            d.wait_send()

    for d in st_out + rec_out:
        d.wait()


def local(*args):
    vm = pltpu.VMEM
    dma = pltpu.SemaphoreType.DMA
    col = (CB, LEV, 8, 128)
    scratch = [
        vm((32, K, 128, 128), BF16), vm(col, F32), vm((CB, LEV - 1, 8, 128), F32),
        vm((8, 512), F32), vm((8, 512), jnp.int32), vm((F, 8, 512), F32), vm((F, 8, 512), F32),
        vm((32, K), jnp.int32), vm((32, K), jnp.int32), vm((32, K), jnp.int32),
        vm((128, 128), F32), vm((512, 128), F32),
        vm((TILES * MSG, 128), F32), vm((TILES * MSG, 128), F32),
        vm((3, CB, F, 8, 128), F32), vm((3, CB, F, 8, 128), F32),
        vm((3, 2, 8, 128), F32), vm((3, 2, 8, 128), F32),
        vm((2, CB, LEV + 8, 128), F32), vm((2, CB, LEV + 8, 128), F32),
        vm((2, 2, CB, LEV, 128), F32), vm((2, 2, CB, LEV, 128), F32),
        vm((5, CB, 8, 128), F32), vm((CB, 8, 128), F32),
        vm(col, F32), vm(col, F32), vm((CB, 8, 128), F32),
        vm((CB, HALF, 8, 128), F32), vm(col, F32), vm(col, F32), vm(col, F32), vm(col, F32),
        vm((CB, F, 8, 128), F32),
        dma((15,)), dma((WCH,)), dma((TILES,)), dma((TILES,)), dma((2, 2)), dma((2, 2)),
        dma((3,)), dma((3,)), dma((3, 2)), dma((3, 2)),
    ]
    any_spec = pl.BlockSpec(memory_space=pl.ANY)
    return pl.pallas_call(
        kernel,
        out_shape=(
            jax.ShapeDtypeStruct((LEV, 8, 512), F32), jax.ShapeDtypeStruct((F, 8, 512), F32),
        ),
        in_specs=[any_spec] * 10,
        out_specs=(any_spec, any_spec),
        scratch_shapes=scratch,
        compiler_params=pltpu.CompilerParams(
            collective_id=0, has_side_effects=True, vmem_limit_bytes=50 * 1024 * 1024
        ),
        name="window",
    )(*args)


def solution(mesh):
    both = ("grp", "tile")
    in_specs = (
        P(None, both, None), P(None, both, None), P(both, None), P("tile", None),
        P(None, both, None), P(None, both, None), P(both, None, None, None),
        P(both, None), P(both, None), P(both, None),
    )
    out_specs = (P(None, both, None), P(None, both, None))
    return jax.shard_map(local, mesh=mesh, in_specs=in_specs, out_specs=out_specs, check_vma=False)
```

time: 112 us -> 45.8 us (0.41)
  the two profiles are of different devices: /device:TPU:6 before, /device:TPU:0 now
where the time goes in v1:
time: 45.8 us; the launch traced here: 45.4 us
  Pallas kernels  35.3 us (77%)
  local copies, waits for them, and re-layouts  9.44 us (21%)
  between operations  0.65 us (1%)
    pallas_call x1, Pallas kernels, local(): pl.pallas_call(kernel, out_shape=(jax.ShapeDtypeStruct((LEV, 8, 512), F32...  35.3 us
    unnamed x17, local copies, waits for them, and re-layouts  9.44 us

profile of v1, /device:TPU:0, one launch (start us, length us, event | category | flops | bytes accessed | tf_op | source)
XLA Modules:
  0.0 45.4 jit_solution(18236743269698015582)
XLA Ops:
  0.6 0.8 %copy.12.dt_h = s32[32,4]{1,0:T(8,128)S(1)} copy(s32[32,4]{0,1:T(4,128)} %param.17) | data formatting | bytes 1024 | tf_op args[7]
  1.4 0.8 %copy.13.db_h = s32[32,4]{1,0:T(8,128)S(1)} copy(s32[32,4]{0,1:T(4,128)} %param.18) | data formatting | bytes 1024 | tf_op args[8]
  2.2 0.8 %copy.14.dg_h = s32[32,4]{1,0:T(8,128)S(1)} copy(s32[32,4]{0,1:T(4,128)} %param.19) | data formatting | bytes 1024 | tf_op args[9]
  2.9 0.0 copy-start
  2.9 1.2 %copy-done = f32[64,8,512]{2,1,0:T(8,128)S(1)} copy-done((f32[64,8,512]{2,1,0:T(8,128)S(1)}, f32[64,8,512]{2,1,0:T(8,128)}, u32[]{:S(2)}) %copy-start) | copy-done | bytes 1048600
  4.1 0.0 copy-start.1
  4.1 1.2 %copy-done.1 = f32[63,8,512]{2,1,0:T(8,128)S(1)} copy-done((f32[63,8,512]{2,1,0:T(8,128)S(1)}, f32[63,8,512]{2,1,0:T(8,128)}, u32[]{:S(2)}) %copy-start.1) | copy-done | bytes 1032216
  5.4 0.0 copy-start.2
  5.4 0.8 %copy-done.2 = f32[4,8,512]{2,1,0:T(8,128)S(1)} copy-done((f32[4,8,512]{2,1,0:T(8,128)S(1)}, f32[4,8,512]{2,1,0:T(8,128)}, u32[]{:S(2)}) %copy-start.2) | copy-done | bytes 65560
  6.2 0.0 copy-start.3
  6.2 0.8 %copy-done.3 = f32[4,8,512]{2,1,0:T(8,128)S(1)} copy-done((f32[4,8,512]{2,1,0:T(8,128)S(1)}, f32[4,8,512]{2,1,0:T(8,128)}, u32[]{:S(2)}) %copy-start.3) | copy-done | bytes 65560
  7.0 0.0 copy-start.4
  7.0 0.7 %copy-done.4 = f32[8,512]{1,0:T(8,128)S(1)} copy-done((f32[8,512]{1,0:T(8,128)S(1)}, f32[8,512]{1,0:T(8,128)}, u32[]{:S(2)}) %copy-start.4) | copy-done | bytes 16408
  7.8 0.0 copy-start.5
  7.8 0.7 %copy-done.5 = s32[8,512]{1,0:T(8,128)S(1)} copy-done((s32[8,512]{1,0:T(8,128)S(1)}, s32[8,512]{1,0:T(8,128)}, u32[]{:S(2)}) %copy-start.5) | copy-done | bytes 16408
  8.5 35.3 %window.1 = (f32[64,8,512]{2,1,0:T(8,128)S(1)}, f32[4,8,512]{2,1,0:T(8,128)S(1)}) custom-call(f32[64,8,512]{2,1,0:T(8,128)S(1)} %copy-done, f32[63,8,512]{2,1,0:T(8,128)S(1)} %copy-done.1, f32[8,512]{1,0:T(8,128)S(1)} %copy-done.4, s32[8,512]{1,0:T(8,128)S(1)} %copy-done.5, f32[4,8,512]{2,1,0:T(8,128)S(1)} %copy-done.2, f32[4,8,512]{2,1,0:T(8,128)S(1)} %copy-done.3, ...), custom_call_target="tpu_custom_call" | custom-call | tf_op jit(solution)/shard_map/window/pallas_call | solution.py:547
  43.8 1.0 %copy.17 = f32[64,8,512]{2,1,0:T(8,128)} copy(f32[64,8,512]{2,1,0:T(8,128)S(1)} %get-tuple-element.4) | data formatting | bytes 2097152
  44.7 0.6 %copy.18 = f32[4,8,512]{2,1,0:T(8,128)} copy(f32[4,8,512]{2,1,0:T(8,128)S(1)} %get-tuple-element.5) | data formatting | bytes 131072
Async XLA Ops:
  2.9 1.2 %copy-start = (f32[64,8,512]{2,1,0:T(8,128)S(1)}, f32[64,8,512]{2,1,0:T(8,128)}, u32[]{:S(2)}) copy-start(f32[64,8,512]{2,1,0:T(8,128)} %state_h.1) | copy-start | bytes 3145732
  4.1 1.2 %copy-start.1 = (f32[63,8,512]{2,1,0:T(8,128)S(1)}, f32[63,8,512]{2,1,0:T(8,128)}, u32[]{:S(2)}) copy-start(f32[63,8,512]{2,1,0:T(8,128)} %vert_h.1) | copy-start | bytes 3096580
  5.4 0.8 %copy-start.2 = (f32[4,8,512]{2,1,0:T(8,128)S(1)}, f32[4,8,512]{2,1,0:T(8,128)}, u32[]{:S(2)}) copy-start(f32[4,8,512]{2,1,0:T(8,128)} %coup_h.1) | copy-start | bytes 196612
  6.2 0.8 %copy-start.3 = (f32[4,8,512]{2,1,0:T(8,128)S(1)}, f32[4,8,512]{2,1,0:T(8,128)}, u32[]{:S(2)}) copy-start(f32[4,8,512]{2,1,0:T(8,128)} %surf_h.1) | copy-start | bytes 196612
  7.0 0.7 %copy-start.4 = (f32[8,512]{1,0:T(8,128)S(1)}, f32[8,512]{1,0:T(8,128)}, u32[]{:S(2)}) copy-start(f32[8,512]{1,0:T(8,128)} %nu_h.1) | copy-start | bytes 49156
  7.8 0.7 %copy-start.5 = (s32[8,512]{1,0:T(8,128)S(1)}, s32[8,512]{1,0:T(8,128)}, u32[]{:S(2)}) copy-start(s32[8,512]{1,0:T(8,128)} %mask_h.1) | copy-start | bytes 49156

commit v2 on v1

--- a/solution.py
+++ b/solution.py
@@ -40,7 +40,7 @@
     out_h, rec_h,
     w_v, st, ve, nu, mask, coup, surf, dt, db, dg,
     xs, terms, slab, got, ps, xr, es, xe,
-    se, re, su, ru, coef, wet, inv, ww, mid, rg, ru_fwd, uu, gg, outv, rv,
+    se, re, su, ru, coef, wet, inv, ww, mid, rg, ru_fwd, uu, gg,
     lsem, wsem, ssem, rsem, hs, hr, xss, xrs, ess, ers,
 ):
     grp = lax.axis_index("grp")
@@ -105,17 +105,16 @@
     k_of = lane % 4
     b_of = 2 * ((lane % 64) // 4) + lane // 64
     group_label = jnp.where(ocean, 32, 0)
-    code = dt[...] * 128 + db[...] + dg[...] * group_label + 1
-    code = code.astype(F32)
-    wide = jnp.zeros((32, 128), F32)
-    for k in range(K):
-        wide = jnp.where(k_of == k, code[:, k:k + 1], wide)
-    code_row = jnp.sum(jnp.where(iota((32, 128), 0) == b_of, wide, 0.0), axis=0, keepdims=True)
-    code_int = code_row.astype(jnp.int32)
-    drel = ((code_int // 128) + TILES - tile) % TILES
-    label = (code_int % 128).astype(F32)
+    both = jnp.concatenate(
+        [((dt[...] + TILES - tile) % TILES).astype(F32),
+         (db[...] + dg[...] * group_label + 1).astype(F32)], axis=0
+    ).astype(BF16)
+    wide = jnp.dot(both, one_hot(iota((32, 128), 0) == b_of), preferred_element_type=F32)
+    of_k = iota((K, 128), 0) == k_of
+    d_row = jnp.sum(jnp.where(of_k, wide[:K], 0.0), axis=0, keepdims=True)
+    label = jnp.sum(jnp.where(of_k, wide[K:], 0.0), axis=0, keepdims=True)
+    drel = d_row.astype(jnp.int32)
     i0, i1 = iota((128, 128), 0), iota((128, 128), 1)
-    d_row = drel.astype(F32)
     d_col = jnp.sum(jnp.where(i0 == i1, d_row, 0.0), axis=1, keepdims=True)
     pos = jnp.sum(jnp.where((d_col == d_row) & (i0 < i1), 1.0, 0.0), axis=0, keepdims=True)
     slot = drel * SLOTS + pos.astype(jnp.int32)
@@ -434,18 +433,11 @@
         tot = None
         for f in range(F):
             r = xr[0, c, f] + xr[1, c, f] + xr[2, c, f]
-            rv[c, f] = r
+            rec_h[f, :, c * 128:(c + 1) * 128] = r
             tot = r if tot is None else tot + r
         forc.append(GAIN * wets[c] * tot)
         f_up.append(e_up[c:c + 1] * wet_up[c])
         f_dn.append(e_dn[c:c + 1] * wet_dn[c])
-    rec_out = [
-        pltpu.make_async_copy(rv.at[c], rec_h.at[:, :, c * 128:(c + 1) * 128], lsem.at[c])
-        for c in range(CB)
-    ]
-    for d in rec_out:
-        d.start()
-
     for d in edge_u:
         d.wait_recv()
 
@@ -487,20 +479,13 @@
         for c in range(CB):
             x0 = inv[c, l_t] * ru_fwd[c, l_t] + ww[c, l_t] * x_t[c]
             x1 = inv[c, l_b] * ru_fwd[c, l_b] + ww[c, l_b] * x_b[c]
-            outv[c, l_t] = x0
-            outv[c, l_b] = x1
+            out_h[l_t, :, c * 128:(c + 1) * 128] = x0
+            out_h[l_b, :, c * 128:(c + 1) * 128] = x1
             n_t.append(x0)
             n_b.append(x1)
         return n_t, n_b
 
     lax.fori_loop(0, HALF, back2, (x_t, x_b), unroll=2)
-    st_out = [
-        pltpu.make_async_copy(outv.at[c], out_h.at[:, :, c * 128:(c + 1) * 128], lsem.at[4 + c])
-        for c in range(CB)
-    ]
-    for d in st_out:
-        d.start()
-
     for d in edge + edge_u:
         d.wait_send()
 
@@ -517,9 +502,6 @@
     def _():
         for d in air_sends():
             d.wait_send()
-
-    for d in st_out + rec_out:
-        d.wait()
 
 
 def local(*args):
@@ -529,7 +511,7 @@
     scratch = [
         vm((32, K, 128, 128), BF16), vm(col, F32), vm((CB, LEV - 1, 8, 128), F32),
         vm((8, 512), F32), vm((8, 512), jnp.int32), vm((F, 8, 512), F32), vm((F, 8, 512), F32),
-        vm((32, K), jnp.int32), vm((32, K), jnp.int32), vm((32, K), jnp.int32),
+        vm((K, 32), jnp.int32), vm((K, 32), jnp.int32), vm((K, 32), jnp.int32),
         vm((128, 128), F32), vm((512, 128), F32),
         vm((TILES * MSG, 128), F32), vm((TILES * MSG, 128), F32),
         vm((3, CB, F, 8, 128), F32), vm((3, CB, F, 8, 128), F32),
@@ -538,25 +520,25 @@
         vm((2, 2, CB, LEV, 128), F32), vm((2, 2, CB, LEV, 128), F32),
         vm((5, CB, 8, 128), F32), vm((CB, 8, 128), F32),
         vm(col, F32), vm(col, F32), vm((CB, 8, 128), F32),
-        vm((CB, HALF, 8, 128), F32), vm(col, F32), vm(col, F32), vm(col, F32), vm(col, F32),
-        vm((CB, F, 8, 128), F32),
+        vm((CB, HALF, 8, 128), F32), vm(col, F32), vm(col, F32), vm(col, F32),
         dma((15,)), dma((WCH,)), dma((TILES,)), dma((TILES,)), dma((2, 2)), dma((2, 2)),
         dma((3,)), dma((3,)), dma((3, 2)), dma((3, 2)),
     ]
-    any_spec = pl.BlockSpec(memory_space=pl.ANY)
+    hbm = pl.BlockSpec(memory_space=pltpu.HBM)
+    out = pl.BlockSpec(memory_space=pltpu.VMEM)
     return pl.pallas_call(
         kernel,
         out_shape=(
-            jax.ShapeDtypeStruct((LEV, 8, 512), F32), jax.ShapeDtypeStruct((F, 8, 512), F32),
+            vm((LEV, 8, 512), F32), vm((F, 8, 512), F32),
         ),
-        in_specs=[any_spec] * 10,
-        out_specs=(any_spec, any_spec),
+        in_specs=[hbm] * 10,
+        out_specs=(out, out),
         scratch_shapes=scratch,
         compiler_params=pltpu.CompilerParams(
             collective_id=0, has_side_effects=True, vmem_limit_bytes=50 * 1024 * 1024
         ),
         name="window",
-    )(*args)
+    )(*(pltpu.with_memory_space_constraint(a, pltpu.HBM) for a in (*args[:7], *(a.T for a in args[7:]))))
 
 
 def solution(mesh):

time: 45.8 us -> 37 us (0.81)
  local copies, waits for them, and re-layouts: 9.44 us -> 1.6 us
  Pallas kernels: 35.3 us -> 34.7 us
    unnamed x17 -> x2, local copies, waits for them, and re-layouts: 9.44 us -> 1.6 us
    pallas_call x1, Pallas kernels: 35.3 us -> 34.7 us  [local(): pl.pallas_call(kernel, out_shape=(vm((LEV, 8, 512), F32), vm((F, 8, 512),...]
where the time goes in v2:
time: 37 us; the launch traced here: 36.9 us
  Pallas kernels  34.7 us (94%)
  local copies, waits for them, and re-layouts  1.6 us (4%)
  between operations  0.64 us (2%)
    pallas_call x1, Pallas kernels, local(): pl.pallas_call(kernel, out_shape=(vm((LEV, 8, 512), F32), vm((F, 8, 512),...  34.7 us
    unnamed x2, local copies, waits for them, and re-layouts  1.6 us

profile of v2, /device:TPU:0, one launch (start us, length us, event | category | flops | bytes accessed | tf_op | source)
XLA Modules:
  0.0 36.9 jit_solution(14859299972387976137)
XLA Ops:
  0.6 34.7 %window.1 = (f32[64,8,512]{2,1,0:T(8,128)S(1)}, f32[4,8,512]{2,1,0:T(8,128)S(1)}) custom-call(f32[64,8,512]{2,1,0:T(8,128)} %state_h.1, f32[63,8,512]{2,1,0:T(8,128)} %vert_h.1, f32[8,512]{1,0:T(8,128)} %nu_h.1, s32[8,512]{1,0:T(8,128)} %mask_h.1, f32[4,8,512]{2,1,0:T(8,128)} %coup_h.1, f32[4,8,512]{2,1,0:T(8,128)} %surf_h.1, bf16[32,4,128,128]{3,2,1,0:T(8,128)(2,1)} %w_h.1, ...), custom_call_target="tpu_custom_call" | custom-call | tf_op jit(solution)/shard_map/window/pallas_call | solution.py:529
  35.3 1.0 %copy.14 = f32[64,8,512]{2,1,0:T(8,128)} copy(f32[64,8,512]{2,1,0:T(8,128)S(1)} %get-tuple-element.2) | data formatting | bytes 2097152
  36.3 0.6 %copy.15 = f32[4,8,512]{2,1,0:T(8,128)} copy(f32[4,8,512]{2,1,0:T(8,128)S(1)} %get-tuple-element.3) | data formatting | bytes 131072

commit v3 on v2

--- a/solution.py
+++ b/solution.py
@@ -17,6 +17,7 @@
 TILES = 32
 SLOTS = 8
 MSG = 40
+SENT = 33
 CB = 4
 WCH = 8
 GAIN = 0.25
@@ -38,7 +39,7 @@
 def kernel(
     state_h, vert_h, nu_h, mask_h, coup_h, surf_h, w_h, dt_h, db_h, dg_h,
     out_h, rec_h,
-    w_v, st, ve, nu, mask, coup, surf, dt, db, dg,
+    w_v, s0, st, ve, nu, mask, coup, surf, dt, db, dg,
     xs, terms, slab, got, ps, xr, es, xe,
     se, re, su, ru, coef, wet, inv, ww, mid, rg, ru_fwd, uu, gg,
     lsem, wsem, ssem, rsem, hs, hr, xss, xrs, ess, ers,
@@ -62,6 +63,7 @@
     small = [
         load(dt_h, dt, 0), load(db_h, db, 1), load(dg_h, dg, 2),
         load(mask_h, mask, 3), load(coup_h, coup, 4), load(surf_h, surf, 5), load(nu_h, nu, 6),
+        load(state_h.at[0], s0, 15),
     ]
     st_load = [load(state_h.at[:, :, c * 128:(c + 1) * 128], st.at[c], 7 + c) for c in range(CB)]
     ve_load = [
@@ -72,7 +74,7 @@
         pltpu.make_async_copy(w_h.at[pl.ds(i * per, per)], w_v.at[pl.ds(i * per, per)], wsem.at[i])
         for i in range(WCH)
     ]
-    for d in small + st_load + w_load + ve_load:
+    for d in small + w_load + st_load + ve_load:
         d.start()
 
     barrier = pltpu.get_barrier_semaphore()
@@ -124,40 +126,13 @@
     for j in range(TILES // 8):
         slab[pl.ds(j * 8 * MSG + 32, 8, stride=MSG), :] = tags[j * 8:(j + 1) * 8]
 
-    for d in st_load:
-        d.wait()
     for c in range(CB):
         cs = slice(c * 128, (c + 1) * 128)
         wet_c = jnp.where(ocean, mask[:, cs].astype(F32), 1.0)
         wet[c] = wet_c
         for f in range(F):
-            send = coup[f, :, cs] * (st[c, 0] - surf[f, :, cs]) * wet_c
+            send = coup[f, :, cs] * (s0[:, cs] - surf[f, :, cs]) * wet_c
             xs[pl.ds(c * 4 + f, 8, stride=16), :] = send
-
-    for c in range(CB):
-        rows = st.at[c].reshape(LEV * 8, 128)
-        for side in range(2):
-            se[side, c, 0:LEV, :] = rows[pl.ds(7 * side, LEV, stride=8), :]
-            se[side, c, LEV:LEV + 8, :] = wet[c]
-
-    @pl.when(ocean)
-    def _():
-        pl.semaphore_wait(barrier, 31 + 2 + 9)
-
-    @pl.when(jnp.logical_not(ocean))
-    def _():
-        pl.semaphore_wait(barrier, 31 + 2 + 3)
-
-    def halo(src, dst, side, i):
-        return pltpu.make_async_remote_copy(
-            src_ref=src.at[side], dst_ref=dst.at[side], send_sem=hs.at[i, side],
-            recv_sem=hr.at[i, side], device_id=above_dev if side == 0 else below_dev,
-            device_id_type=MESH,
-        )
-
-    edge = [halo(se, re, side, 0) for side in range(2)]
-    for d in edge:
-        d.start()
 
     row8 = iota((8, 128), 0)
 
@@ -186,9 +161,17 @@
     hi = jnp.concatenate(his, axis=1)
     lo = jnp.concatenate(los, axis=1)
 
+    @pl.when(ocean)
+    def _():
+        pl.semaphore_wait(barrier, 31 + 2 + 9)
+
+    @pl.when(jnp.logical_not(ocean))
+    def _():
+        pl.semaphore_wait(barrier, 31 + 2 + 3)
+
     def a2a(d):
         return pltpu.make_async_remote_copy(
-            src_ref=slab.at[pl.ds(d * MSG, MSG)], dst_ref=got.at[pl.ds(d * MSG, MSG)],
+            src_ref=slab.at[pl.ds(d * MSG, SENT)], dst_ref=got.at[pl.ds(d * MSG, SENT)],
             send_sem=ssem.at[d], recv_sem=rsem.at[d],
             device_id=(grp, (tile + d) % TILES), device_id_type=MESH,
         )
@@ -210,6 +193,25 @@
         @pl.loop(max(1, p * (TILES // parts)), (p + 1) * (TILES // parts))
         def _(d):
             a2a(d).start()
+
+    for d in st_load:
+        d.wait()
+    for c in range(CB):
+        rows = st.at[c].reshape(LEV * 8, 128)
+        for side in range(2):
+            se[side, c, 0:LEV, :] = rows[pl.ds(7 * side, LEV, stride=8), :]
+            se[side, c, LEV:LEV + 8, :] = wet[c]
+
+    def halo(src, dst, side, i):
+        return pltpu.make_async_remote_copy(
+            src_ref=src.at[side], dst_ref=dst.at[side], send_sem=hs.at[i, side],
+            recv_sem=hr.at[i, side], device_id=above_dev if side == 0 else below_dev,
+            device_id_type=MESH,
+        )
+
+    edge = [halo(se, re, side, 0) for side in range(2)]
+    for d in edge:
+        d.start()
 
     for d in ve_load:
         d.wait()
@@ -239,7 +241,7 @@
 
     ones = [one] * CB
     zeros = [zero] * CB
-    e_t, _, e_b, r_g = lax.fori_loop(0, HALF, factor, (ones, ones, ones, ones), unroll=2)
+    e_t, _, e_b, r_g = lax.fori_loop(0, HALF, factor, (ones, ones, ones, ones), unroll=4)
     mids = [1.0 / (e_t[c] + e_b[c] - 1.0) for c in range(CB)]
     for c in range(CB):
         mid[c] = mids[c]
@@ -306,7 +308,7 @@
             n_b.append(ww[c, l_b] * s)
         return n_t, n_b
 
-    r_t, _ = lax.fori_loop(0, HALF, first, (zeros, zeros))
+    r_t, _ = lax.fori_loop(0, HALF, first, (zeros, zeros), unroll=4)
     x_b, x_t, y_b, y_t = [], [], [], []
     for c in range(CB):
         x32 = (ru_fwd[c, HALF] + r_t[c]) * mids[c]
@@ -334,7 +336,7 @@
                 a.append(v)
         return tuple(n)
 
-    lax.fori_loop(0, HALF, back, (x_t, x_b, y_t, y_b), unroll=2)
+    lax.fori_loop(0, HALF, back, (x_t, x_b, y_t, y_b), unroll=4)
 
     for c in range(CB):
         rows_u = uu.at[c].reshape(LEV * 8, 128)
@@ -465,7 +467,7 @@
             n_b.append(ww[c, l_b] * s)
         return n_t, n_b
 
-    r_t, _ = lax.fori_loop(0, HALF, second, (forc, zeros))
+    r_t, _ = lax.fori_loop(0, HALF, second, (forc, zeros), unroll=4)
     x_t, x_b = [], []
     for c in range(CB):
         x32 = (ru_fwd[c, HALF] + r_t[c]) * mid[c]
@@ -485,7 +487,7 @@
             n_b.append(x1)
         return n_t, n_b
 
-    lax.fori_loop(0, HALF, back2, (x_t, x_b), unroll=2)
+    lax.fori_loop(0, HALF, back2, (x_t, x_b), unroll=8)
     for d in edge + edge_u:
         d.wait_send()
 
@@ -509,7 +511,7 @@
     dma = pltpu.SemaphoreType.DMA
     col = (CB, LEV, 8, 128)
     scratch = [
-        vm((32, K, 128, 128), BF16), vm(col, F32), vm((CB, LEV - 1, 8, 128), F32),
+        vm((32, K, 128, 128), BF16), vm((8, 512), F32), vm(col, F32), vm((CB, LEV - 1, 8, 128), F32),
         vm((8, 512), F32), vm((8, 512), jnp.int32), vm((F, 8, 512), F32), vm((F, 8, 512), F32),
         vm((K, 32), jnp.int32), vm((K, 32), jnp.int32), vm((K, 32), jnp.int32),
         vm((128, 128), F32), vm((512, 128), F32),
@@ -521,7 +523,7 @@
         vm((5, CB, 8, 128), F32), vm((CB, 8, 128), F32),
         vm(col, F32), vm(col, F32), vm((CB, 8, 128), F32),
         vm((CB, HALF, 8, 128), F32), vm(col, F32), vm(col, F32), vm(col, F32),
-        dma((15,)), dma((WCH,)), dma((TILES,)), dma((TILES,)), dma((2, 2)), dma((2, 2)),
+        dma((16,)), dma((WCH,)), dma((TILES,)), dma((TILES,)), dma((2, 2)), dma((2, 2)),
         dma((3,)), dma((3,)), dma((3, 2)), dma((3, 2)),
     ]
     hbm = pl.BlockSpec(memory_space=pltpu.HBM)

time: 37 us -> 33.5 us (0.905)
  Pallas kernels: 34.7 us -> 31.2 us
    pallas_call x1, Pallas kernels: 34.7 us -> 31.2 us  [local(): pl.pallas_call(kernel, out_shape=(vm((LEV, 8, 512), F32), vm((F, 8, 512),...]
where the time goes in v3:
time: 33.5 us; the launch traced here: 33.4 us
  Pallas kernels  31.2 us (93%)
  local copies, waits for them, and re-layouts  1.6 us (5%)
  between operations  0.64 us (2%)
    pallas_call x1, Pallas kernels, local(): pl.pallas_call(kernel, out_shape=(vm((LEV, 8, 512), F32), vm((F, 8, 512),...  31.2 us
    unnamed x2, local copies, waits for them, and re-layouts  1.6 us

profile of v3, /device:TPU:0, one launch (start us, length us, event | category | flops | bytes accessed | tf_op | source)
XLA Modules:
  0.0 33.4 jit_solution(17955245318459424551)
XLA Ops:
  0.6 31.2 %window.1 = (f32[64,8,512]{2,1,0:T(8,128)S(1)}, f32[4,8,512]{2,1,0:T(8,128)S(1)}) custom-call(f32[64,8,512]{2,1,0:T(8,128)} %state_h.1, f32[63,8,512]{2,1,0:T(8,128)} %vert_h.1, f32[8,512]{1,0:T(8,128)} %nu_h.1, s32[8,512]{1,0:T(8,128)} %mask_h.1, f32[4,8,512]{2,1,0:T(8,128)} %coup_h.1, f32[4,8,512]{2,1,0:T(8,128)} %surf_h.1, bf16[32,4,128,128]{3,2,1,0:T(8,128)(2,1)} %w_h.1, ...), custom_call_target="tpu_custom_call" | custom-call | tf_op jit(solution)/shard_map/window/pallas_call | solution.py:531
  31.8 1.0 %copy.14 = f32[64,8,512]{2,1,0:T(8,128)} copy(f32[64,8,512]{2,1,0:T(8,128)S(1)} %get-tuple-element.2) | data formatting | bytes 2097152
  32.8 0.6 %copy.15 = f32[4,8,512]{2,1,0:T(8,128)} copy(f32[4,8,512]{2,1,0:T(8,128)S(1)} %get-tuple-element.3) | data formatting | bytes 131072

commit v4 on v3

--- a/solution.py
+++ b/solution.py
@@ -20,6 +20,7 @@
 SENT = 33
 CB = 4
 WCH = 8
+HR = 3 * LEV + 8
 GAIN = 0.25
 
 
@@ -41,7 +42,7 @@
     out_h, rec_h,
     w_v, s0, st, ve, nu, mask, coup, surf, dt, db, dg,
     xs, terms, slab, got, ps, xr, es, xe,
-    se, re, su, ru, coef, wet, inv, ww, mid, rg, ru_fwd, uu, gg,
+    se, re, xh, coef, coef_h, wet, inv, ww, mid, rg, ru_fwd, uu, gg,
     lsem, wsem, ssem, rsem, hs, hr, xss, xrs, ess, ers,
 ):
     grp = lax.axis_index("grp")
@@ -56,6 +57,29 @@
     above_dev = dev_id((dev + n_dev - 1) % n_dev)
     below_dev = dev_id((dev + 1) % n_dev)
     t_prev, t_next = (tile + TILES - 1) % TILES, (tile + 1) % TILES
+
+    barrier = pltpu.get_barrier_semaphore()
+
+    def tell(device):
+        pl.semaphore_signal(barrier, inc=1, device_id=device, device_id_type=MESH)
+
+    @pl.loop(1, TILES)
+    def _(d):
+        tell((grp, (tile + d) % TILES))
+
+    tell(above_dev)
+    tell(below_dev)
+
+    @pl.when(ocean)
+    def _():
+        for g in range(3):
+            for t in (tile, t_prev, t_next):
+                tell((g, t))
+
+    @pl.when(jnp.logical_not(ocean))
+    def _():
+        for t in (tile, t_prev, t_next):
+            tell((3, t))
 
     def load(src, dst, i):
         return pltpu.make_async_copy(src, dst, lsem.at[i])
@@ -76,29 +100,6 @@
     ]
     for d in small + w_load + st_load + ve_load:
         d.start()
-
-    barrier = pltpu.get_barrier_semaphore()
-
-    def tell(device):
-        pl.semaphore_signal(barrier, inc=1, device_id=device, device_id_type=MESH)
-
-    @pl.loop(1, TILES)
-    def _(d):
-        tell((grp, (tile + d) % TILES))
-
-    tell(above_dev)
-    tell(below_dev)
-
-    @pl.when(ocean)
-    def _():
-        for g in range(3):
-            for t in (tile, t_prev, t_next):
-                tell((g, t))
-
-    @pl.when(jnp.logical_not(ocean))
-    def _():
-        for t in (tile, t_prev, t_next):
-            tell((3, t))
 
     for d in small:
         d.wait()
@@ -161,14 +162,6 @@
     hi = jnp.concatenate(his, axis=1)
     lo = jnp.concatenate(los, axis=1)
 
-    @pl.when(ocean)
-    def _():
-        pl.semaphore_wait(barrier, 31 + 2 + 9)
-
-    @pl.when(jnp.logical_not(ocean))
-    def _():
-        pl.semaphore_wait(barrier, 31 + 2 + 3)
-
     def a2a(d):
         return pltpu.make_async_remote_copy(
             src_ref=slab.at[pl.ds(d * MSG, SENT)], dst_ref=got.at[pl.ds(d * MSG, SENT)],
@@ -190,31 +183,51 @@
                     j * 8:(j + 1) * 8, f * 128:(f + 1) * 128
                 ]
 
-        @pl.loop(max(1, p * (TILES // parts)), (p + 1) * (TILES // parts))
-        def _(d):
-            a2a(d).start()
-
-    for d in st_load:
+    for d in st_load + ve_load:
         d.wait()
     for c in range(CB):
         rows = st.at[c].reshape(LEV * 8, 128)
+        rows_v = ve.at[c].reshape((LEV - 1) * 8, 128)
         for side in range(2):
-            se[side, c, 0:LEV, :] = rows[pl.ds(7 * side, LEV, stride=8), :]
-            se[side, c, LEV:LEV + 8, :] = wet[c]
-
-    def halo(src, dst, side, i):
+            near, far = 7 * side, 1 + 5 * side
+            se[side, c, 0:LEV, :] = rows[pl.ds(near, LEV, stride=8), :]
+            se[side, c, LEV:2 * LEV, :] = rows[pl.ds(far, LEV, stride=8), :]
+            se[side, c, 2 * LEV:3 * LEV - 1, :] = rows_v[pl.ds(near, LEV - 1, stride=8), :]
+            se[side, c, 3 * LEV:3 * LEV + 1, :] = wet[c, near:near + 1, :]
+            se[side, c, 3 * LEV + 1:3 * LEV + 2, :] = wet[c, far:far + 1, :]
+            se[side, c, 3 * LEV + 2:3 * LEV + 3, :] = nu[near:near + 1, c * 128:(c + 1) * 128]
+
+    def halo(side):
         return pltpu.make_async_remote_copy(
-            src_ref=src.at[side], dst_ref=dst.at[side], send_sem=hs.at[i, side],
-            recv_sem=hr.at[i, side], device_id=above_dev if side == 0 else below_dev,
+            src_ref=se.at[side], dst_ref=re.at[side], send_sem=hs.at[side],
+            recv_sem=hr.at[side], device_id=above_dev if side == 0 else below_dev,
             device_id_type=MESH,
         )
 
-    edge = [halo(se, re, side, 0) for side in range(2)]
-    for d in edge:
-        d.start()
-
-    for d in ve_load:
-        d.wait()
+    @pl.when(ocean)
+    def _():
+        pl.semaphore_wait(barrier, 31 + 2 + 9)
+
+    @pl.when(jnp.logical_not(ocean))
+    def _():
+        pl.semaphore_wait(barrier, 31 + 2 + 3)
+
+    @pl.loop(1, TILES)
+    def _(d):
+        a2a(d).start()
+
+    edge = [halo(side) for side in range(2)]
+    to_above, to_below = (dev != 0) & (dev != 96), (dev != 127) & (dev != 95)
+    from_above, from_below = (dev != 0) & (dev != 96), (dev != 127) & (dev != 95)
+
+    @pl.when(to_above)
+    def _():
+        edge[0].start()
+
+    @pl.when(to_below)
+    def _():
+        edge[1].start()
+
     inv[0, 0] = jnp.ones((8, 128), F32)
     inv[0, 1] = jnp.zeros((8, 128), F32)
     one, zero = inv[0, 0], inv[0, 1]
@@ -246,8 +259,107 @@
     for c in range(CB):
         mid[c] = mids[c]
 
-    for d in edge:
-        d.wait_recv()
+    y_t, y_b = [], []
+    for c in range(CB):
+        y_t.append(r_g[c] * mids[c])
+        y_b.append(inv[c, HALF - 1] * rg[c, HALF - 1] + ww[c, HALF - 1] * y_t[c])
+
+    def back_g(i, carry):
+        y_t, y_b = carry
+        l_t, l_b = HALF - 1 - i, HALF + i
+        n_t, n_b = [], []
+        for c in range(CB):
+            y0 = inv[c, l_t] * rg[c, l_t] + ww[c, l_t] * y_t[c]
+            y1 = ww[c, l_b] * y_b[c]
+            gg[c, l_t] = y0
+            gg[c, l_b] = y1
+            n_t.append(y0)
+            n_b.append(y1)
+        return n_t, n_b
+
+    lax.fori_loop(0, HALF, back_g, (y_t, y_b), unroll=4)
+
+    got[0:MSG, :] = slab[0:MSG, :]
+
+    @pl.loop(1, TILES)
+    def _(d):
+        a2a(d).wait_recv()
+
+    halves = []
+    for h in range(2):
+        t = got[pl.ds(h * 16 * MSG + 32, 8, stride=MSG), :] + got[
+            pl.ds((h * 16 + 8) * MSG + 32, 8, stride=MSG), :
+        ]
+        halves.append(jnp.sum(t, axis=0, keepdims=True))
+    tag_row = jnp.concatenate(halves, axis=1)
+    m = iota((96, 256), 0)
+    want = (m // 32) * 32 + (m % 8) * 4 + (m % 32) // 8 + 1
+    ch2 = one_hot(want.astype(F32) == tag_row)
+    for f in range(F):
+        items = jnp.concatenate(
+            [got[d * MSG + f * 8:d * MSG + f * 8 + 8, :] for d in range(TILES)], axis=0
+        )
+        hi, lo = split(items)
+        part = jnp.dot(ch2, hi, preferred_element_type=F32) + jnp.dot(
+            ch2, lo, preferred_element_type=F32
+        )
+        for g in range(3):
+            for c in range(CB):
+                ps[g, c, f] = part[g * 32 + c * 8:g * 32 + c * 8 + 8]
+    for g in range(3):
+        for c in range(CB):
+            tot = ps[g, c, 0] + ps[g, c, 1] + ps[g, c, 2] + ps[g, c, 3]
+            es[g, 0, c:c + 1, :] = tot[0:1]
+            es[g, 1, c:c + 1, :] = tot[7:8]
+
+    def across(g, src, to, j):
+        return pltpu.make_async_remote_copy(
+            src_ref=src, dst_ref=xr.at[j], send_sem=xss.at[g], recv_sem=xrs.at[j],
+            device_id=to, device_id_type=MESH,
+        )
+
+    def across_edge(g, side, to, j):
+        return pltpu.make_async_remote_copy(
+            src_ref=es.at[g, side], dst_ref=xe.at[j, side], send_sem=ess.at[g, side],
+            recv_sem=ers.at[j, side], device_id=to, device_id_type=MESH,
+        )
+
+    def ocean_sends():
+        copies = []
+        for g in range(3):
+            copies.append(across_edge(g, 0, dev_id((g * TILES + tile + 95) % 96), 0))
+            copies.append(across_edge(g, 1, dev_id((g * TILES + tile + 1) % 96), 0))
+            copies.append(across(g, ps.at[g], (g, tile), 0))
+        return copies
+
+    def air_sends():
+        return [
+            across_edge(0, 0, (3, t_prev), grp),
+            across_edge(0, 1, (3, t_next), grp),
+            across(0, ps.at[0], (3, tile), grp),
+        ]
+
+    @pl.when(ocean)
+    def _():
+        for d in ocean_sends():
+            d.start()
+
+    @pl.when(jnp.logical_not(ocean))
+    def _():
+        for d in air_sends():
+            d.start()
+        for j in range(1, 3):
+            xr[j] = jnp.zeros(xr.shape[1:], F32)
+            xe[j] = jnp.zeros(xe.shape[1:], F32)
+
+    @pl.when(from_below)
+    def _():
+        edge[0].wait_recv()
+
+    @pl.when(from_above)
+    def _():
+        edge[1].wait_recv()
+
     lane8 = iota((8, 128), 1)
     keep_above = jnp.where((dev != 0) & (dev != 96), 1.0, 0.0)
     keep_below = jnp.where((dev != 127) & (dev != 95), 1.0, 0.0)
@@ -264,8 +376,8 @@
             out.append((left, right, above, below))
         return out
 
-    wet_up = [re[1, c, LEV + 7:LEV + 8, :] for c in range(CB)]
-    wet_dn = [re[0, c, LEV:LEV + 1, :] for c in range(CB)]
+    wet_up = [re[1, c, 3 * LEV:3 * LEV + 1, :] for c in range(CB)]
+    wet_dn = [re[0, c, 3 * LEV:3 * LEV + 1, :] for c in range(CB)]
     around = neighbours(
         wets, [w * keep_above for w in wet_up], [w * keep_below for w in wet_dn]
     )
@@ -290,128 +402,102 @@
             out.append(total)
         return out
 
-    def halo_rows(ref, l):
-        return [ref[c, pl.ds(l, 1), :] for c in range(CB)]
+    re_rows = re.reshape(2 * CB * HR, 128)
+    se_rows = se.reshape(2 * CB * HR, 128)
+
+    def theirs(row):
+        return re_rows[pl.ds(row, 8, stride=HR), :]
+
+    def mine(row):
+        return pltpu.roll(se_rows[pl.ds(row, 8, stride=HR), :], 4, 0)
+
+    def sideways(x):
+        left, right = pltpu.roll(x, 1, 1), pltpu.roll(x, 127, 1)
+        left = jnp.where(lane8 == 0, pltpu.roll(left, 1, 0), left)
+        right = jnp.where(lane8 == 127, pltpu.roll(right, 7, 0), right)
+        return left, right
+
+    wet_h = theirs(3 * LEV)
+    left, right = sideways(wet_h)
+    left = jnp.where((lane8 == 0) & (row8 % 4 == 0), 0.0, left)
+    right = jnp.where((lane8 == 127) & (row8 % 4 == 3), 0.0, right)
+    scale = theirs(3 * LEV + 2) * wet_h
+    ch = [scale * left, scale * right, scale * theirs(3 * LEV + 1), scale * mine(3 * LEV)]
+    ch.append(1.0 - (ch[0] + ch[1] + ch[2] + ch[3]))
+    for j in range(5):
+        coef_h[j] = ch[j]
+
+    def spread_h(l):
+        x = theirs(l)
+        left, right = sideways(x)
+        return (
+            coef_h[4] * x + coef_h[0] * left + coef_h[1] * right
+            + coef_h[2] * theirs(LEV + l) + coef_h[3] * mine(l)
+        )
+
+    def halo_rows(side, l):
+        return [re[side, c, pl.ds(l, 1), :] for c in range(CB)]
 
     def first(i, carry):
-        r_t, r_b = carry
+        r_t, r_b, e_t, e_b, _, r_g = carry
         l_t, l_b = i, LEV - 1 - i
-        h_t = spread([st[c, l_t] for c in range(CB)], halo_rows(re.at[1], l_t), halo_rows(re.at[0], l_t))
-        h_b = spread([st[c, l_b] for c in range(CB)], halo_rows(re.at[1], l_b), halo_rows(re.at[0], l_b))
+        a_t = theirs(2 * LEV + i) * wet_h
+        a_b = theirs(3 * LEV - 2 - i) * wet_h
+        i_t = 1.0 / (e_t + a_t)
+        i_b = 1.0 / (e_b + a_b)
+        w_t, w_b = a_t * i_t, a_b * i_b
+        inv[CB, l_t] = i_t
+        inv[CB, l_b] = i_b
+        ww[CB, l_t] = w_t
+        ww[CB, l_b] = w_b
+        rg[CB, l_t] = r_g
+        h_t = spread([st[c, l_t] for c in range(CB)], halo_rows(1, l_t), halo_rows(0, l_t))
+        h_b = spread([st[c, l_b] for c in range(CB)], halo_rows(1, l_b), halo_rows(0, l_b))
+        h_t.append(spread_h(l_t))
+        h_b.append(spread_h(l_b))
         n_t, n_b = [], []
-        for c in range(CB):
+        for c in range(CB + 1):
             r = h_t[c] + r_t[c]
             s = h_b[c] + r_b[c]
             ru_fwd[c, l_t] = r
             ru_fwd[c, l_b] = s
-            n_t.append(ww[c, l_t] * r)
-            n_b.append(ww[c, l_b] * s)
-        return n_t, n_b
-
-    r_t, _ = lax.fori_loop(0, HALF, first, (zeros, zeros), unroll=4)
-    x_b, x_t, y_b, y_t = [], [], [], []
-    for c in range(CB):
-        x32 = (ru_fwd[c, HALF] + r_t[c]) * mids[c]
-        y32 = r_g[c] * mids[c]
-        x_t.append(x32)
-        y_t.append(y32)
-        x_b.append(inv[c, HALF - 1] * ru_fwd[c, HALF - 1] + ww[c, HALF - 1] * x32)
-        y_b.append(inv[c, HALF - 1] * rg[c, HALF - 1] + ww[c, HALF - 1] * y32)
+            n_t.append((ww[c, l_t] if c < CB else w_t) * r)
+            n_b.append((ww[c, l_b] if c < CB else w_b) * s)
+        return n_t, n_b, 1.0 + w_t * e_t, 1.0 + w_b * e_b, e_b, w_t * r_g
+
+    r_t, _, e_t, _, e_b, r_g = lax.fori_loop(
+        0, HALF, first, (zeros + [zero], zeros + [zero], one, one, one, one), unroll=4
+    )
+    mid_h = 1.0 / (e_t + e_b - 1.0)
+    x_b, x_t = [], []
+    for c in range(CB + 1):
+        x_t.append((ru_fwd[c, HALF] + r_t[c]) * (mids[c] if c < CB else mid_h))
+        x_b.append(inv[c, HALF - 1] * ru_fwd[c, HALF - 1] + ww[c, HALF - 1] * x_t[c])
+    y_t = r_g * mid_h
+    y_b = inv[CB, HALF - 1] * rg[CB, HALF - 1] + ww[CB, HALF - 1] * y_t
 
     def back(i, carry):
         x_t, x_b, y_t, y_b = carry
         l_t, l_b = HALF - 1 - i, HALF + i
-        n = [[], [], [], []]
-        for c in range(CB):
+        n_t, n_b = [], []
+        for c in range(CB + 1):
             w_t, w_b, i_t, i_b = ww[c, l_t], ww[c, l_b], inv[c, l_t], inv[c, l_b]
             x0 = i_t * ru_fwd[c, l_t] + w_t * x_t[c]
             x1 = i_b * ru_fwd[c, l_b] + w_b * x_b[c]
-            y0 = i_t * rg[c, l_t] + w_t * y_t[c]
-            y1 = w_b * y_b[c]
             uu[c, l_t] = x0
             uu[c, l_b] = x1
-            gg[c, l_t] = y0
-            gg[c, l_b] = y1
-            for a, v in zip(n, (x0, x1, y0, y1)):
-                a.append(v)
-        return tuple(n)
+            n_t.append(x0)
+            n_b.append(x1)
+        y0 = i_t * rg[CB, l_t] + w_t * y_t
+        y1 = w_b * y_b
+        gg[CB, l_t] = y0
+        gg[CB, l_b] = y1
+        return n_t, n_b, y0, y1
 
     lax.fori_loop(0, HALF, back, (x_t, x_b, y_t, y_b), unroll=4)
 
-    for c in range(CB):
-        rows_u = uu.at[c].reshape(LEV * 8, 128)
-        rows_g = gg.at[c].reshape(LEV * 8, 128)
-        for side in range(2):
-            su[side, 0, c] = rows_u[pl.ds(7 * side, LEV, stride=8), :]
-            su[side, 1, c] = rows_g[pl.ds(7 * side, LEV, stride=8), :]
-    edge_u = [halo(su, ru, side, 1) for side in range(2)]
-    for d in edge_u:
-        d.start()
-
-    got[0:MSG, :] = slab[0:MSG, :]
-
-    @pl.loop(1, TILES)
-    def _(d):
-        a2a(d).wait_recv()
-
-    halves = []
-    for h in range(2):
-        t = got[pl.ds(h * 16 * MSG + 32, 8, stride=MSG), :] + got[
-            pl.ds((h * 16 + 8) * MSG + 32, 8, stride=MSG), :
-        ]
-        halves.append(jnp.sum(t, axis=0, keepdims=True))
-    tag_row = jnp.concatenate(halves, axis=1)
-    m = iota((96, 256), 0)
-    want = (m // 32) * 32 + (m % 8) * 4 + (m % 32) // 8 + 1
-    ch2 = one_hot(want.astype(F32) == tag_row)
-    for f in range(F):
-        items = jnp.concatenate(
-            [got[d * MSG + f * 8:d * MSG + f * 8 + 8, :] for d in range(TILES)], axis=0
-        )
-        hi, lo = split(items)
-        part = jnp.dot(ch2, hi, preferred_element_type=F32) + jnp.dot(
-            ch2, lo, preferred_element_type=F32
-        )
-        for g in range(3):
-            for c in range(CB):
-                ps[g, c, f] = part[g * 32 + c * 8:g * 32 + c * 8 + 8]
-    for g in range(3):
-        for c in range(CB):
-            tot = ps[g, c, 0] + ps[g, c, 1] + ps[g, c, 2] + ps[g, c, 3]
-            es[g, 0, c:c + 1, :] = tot[0:1]
-            es[g, 1, c:c + 1, :] = tot[7:8]
-
-    def across(g, src, to, j):
-        return pltpu.make_async_remote_copy(
-            src_ref=src, dst_ref=xr.at[j], send_sem=xss.at[g], recv_sem=xrs.at[j],
-            device_id=to, device_id_type=MESH,
-        )
-
-    def across_edge(g, side, to, j):
-        return pltpu.make_async_remote_copy(
-            src_ref=es.at[g, side], dst_ref=xe.at[j, side], send_sem=ess.at[g, side],
-            recv_sem=ers.at[j, side], device_id=to, device_id_type=MESH,
-        )
-
-    def ocean_sends():
-        copies = []
-        for g in range(3):
-            copies.append(across_edge(g, 0, dev_id((g * TILES + tile + 95) % 96), 0))
-            copies.append(across_edge(g, 1, dev_id((g * TILES + tile + 1) % 96), 0))
-            copies.append(across(g, ps.at[g], (g, tile), 0))
-        return copies
-
-    def air_sends():
-        return [
-            across_edge(0, 0, (3, t_prev), grp),
-            across_edge(0, 1, (3, t_next), grp),
-            across(0, ps.at[0], (3, tile), grp),
-        ]
-
     @pl.when(ocean)
     def _():
-        for d in ocean_sends():
-            d.start()
         for j in range(3):
             across(j, ps.at[0], (0, tile), j).wait_recv()
             for side in range(2):
@@ -419,16 +505,11 @@
 
     @pl.when(jnp.logical_not(ocean))
     def _():
-        for d in air_sends():
-            d.start()
-        for j in range(1, 3):
-            xr[j] = jnp.zeros(xr.shape[1:], F32)
-            xe[j] = jnp.zeros(xe.shape[1:], F32)
         across(0, ps.at[0], (3, tile), 0).wait_recv()
         for side in range(2):
             across_edge(0, side, (3, tile), 0).wait_recv()
 
-    forc, f_up, f_dn = [], [], []
+    forc = []
     e_up = (xe[0, 1] + xe[1, 1] + xe[2, 1]) * GAIN
     e_dn = (xe[0, 0] + xe[1, 0] + xe[2, 0]) * GAIN
     for c in range(CB):
@@ -438,19 +519,15 @@
             rec_h[f, :, c * 128:(c + 1) * 128] = r
             tot = r if tot is None else tot + r
         forc.append(GAIN * wets[c] * tot)
-        f_up.append(e_up[c:c + 1] * wet_up[c])
-        f_dn.append(e_dn[c:c + 1] * wet_dn[c])
-    for d in edge_u:
-        d.wait_recv()
+    f_h = jnp.where(row8 < 4, e_dn, pltpu.roll(e_up, 4, 0)) * wet_h
+    for l in range(LEV):
+        xh[l] = uu[CB, l] + gg[CB, l] * f_h
+
 
     def level(l):
         x = [uu[c, l] + gg[c, l] * forc[c] for c in range(CB)]
-        up = [
-            ru[1, 0, c, pl.ds(l, 1), :] + ru[1, 1, c, pl.ds(l, 1), :] * f_up[c] for c in range(CB)
-        ]
-        dn = [
-            ru[0, 0, c, pl.ds(l, 1), :] + ru[0, 1, c, pl.ds(l, 1), :] * f_dn[c] for c in range(CB)
-        ]
+        up = [xh[l, 4 + c:5 + c, :] for c in range(CB)]
+        dn = [xh[l, c:c + 1, :] for c in range(CB)]
         return spread(x, up, dn)
 
     def second(i, carry):
@@ -488,8 +565,14 @@
         return n_t, n_b
 
     lax.fori_loop(0, HALF, back2, (x_t, x_b), unroll=8)
-    for d in edge + edge_u:
-        d.wait_send()
+    @pl.when(to_above)
+    def _():
+        edge[0].wait_send()
+
+    @pl.when(to_below)
+    def _():
+        edge[1].wait_send()
+
 
     @pl.loop(1, TILES)
     def _(d):
@@ -504,12 +587,24 @@
     def _():
         for d in air_sends():
             d.wait_send()
+
+
+def flush(state_v, received_v, state_h, received_h, sem):
+    copies = [
+        pltpu.make_async_copy(state_v, state_h, sem.at[0]),
+        pltpu.make_async_copy(received_v, received_h, sem.at[1]),
+    ]
+    for d in copies:
+        d.start()
+    for d in copies:
+        d.wait()
 
 
 def local(*args):
     vm = pltpu.VMEM
     dma = pltpu.SemaphoreType.DMA
     col = (CB, LEV, 8, 128)
+    five = (CB + 1, LEV, 8, 128)
     scratch = [
         vm((32, K, 128, 128), BF16), vm((8, 512), F32), vm(col, F32), vm((CB, LEV - 1, 8, 128), F32),
         vm((8, 512), F32), vm((8, 512), jnp.int32), vm((F, 8, 512), F32), vm((F, 8, 512), F32),
@@ -518,17 +613,16 @@
         vm((TILES * MSG, 128), F32), vm((TILES * MSG, 128), F32),
         vm((3, CB, F, 8, 128), F32), vm((3, CB, F, 8, 128), F32),
         vm((3, 2, 8, 128), F32), vm((3, 2, 8, 128), F32),
-        vm((2, CB, LEV + 8, 128), F32), vm((2, CB, LEV + 8, 128), F32),
-        vm((2, 2, CB, LEV, 128), F32), vm((2, 2, CB, LEV, 128), F32),
-        vm((5, CB, 8, 128), F32), vm((CB, 8, 128), F32),
-        vm(col, F32), vm(col, F32), vm((CB, 8, 128), F32),
-        vm((CB, HALF, 8, 128), F32), vm(col, F32), vm(col, F32), vm(col, F32),
-        dma((16,)), dma((WCH,)), dma((TILES,)), dma((TILES,)), dma((2, 2)), dma((2, 2)),
+        vm((2, CB, HR, 128), F32), vm((2, CB, HR, 128), F32), vm((LEV, 8, 128), F32),
+        vm((5, CB, 8, 128), F32), vm((5, 8, 128), F32), vm((CB, 8, 128), F32),
+        vm(five, F32), vm(five, F32), vm((CB, 8, 128), F32),
+        vm((CB + 1, HALF, 8, 128), F32), vm(five, F32), vm(five, F32), vm(five, F32),
+        dma((16,)), dma((WCH,)), dma((TILES,)), dma((TILES,)), dma((2,)), dma((2,)),
         dma((3,)), dma((3,)), dma((3, 2)), dma((3, 2)),
     ]
     hbm = pl.BlockSpec(memory_space=pltpu.HBM)
     out = pl.BlockSpec(memory_space=pltpu.VMEM)
-    return pl.pallas_call(
+    outs = pl.pallas_call(
         kernel,
         out_shape=(
             vm((LEV, 8, 512), F32), vm((F, 8, 512), F32),
@@ -541,6 +635,16 @@
         ),
         name="window",
     )(*(pltpu.with_memory_space_constraint(a, pltpu.HBM) for a in (*args[:7], *(a.T for a in args[7:]))))
+    return pl.pallas_call(
+        flush,
+        out_shape=(
+            jax.ShapeDtypeStruct((LEV, 8, 512), F32), jax.ShapeDtypeStruct((F, 8, 512), F32),
+        ),
+        in_specs=[pl.BlockSpec(memory_space=pltpu.VMEM)] * 2,
+        out_specs=(hbm, hbm),
+        scratch_shapes=[dma((2,))],
+        name="flush",
+    )(*(pltpu.with_memory_space_constraint(a, pltpu.VMEM) for a in outs))
 
 
 def solution(mesh):

time: 33.5 us -> 30.1 us (0.90)
  the two profiles are of different devices: /device:TPU:0 before, /device:TPU:6 now
where the time goes in v4:
time: 30.1 us; the launch traced here: 30 us
  Pallas kernels  29.4 us (98%)
  between operations  0.64 us (2%)
    pallas_call x1, Pallas kernels, local(): pl.pallas_call(kernel, out_shape=(vm((LEV, 8, 512), F32), vm((F, 8, 512),...  28.4 us
    pallas_call x1, Pallas kernels, local(): pl.pallas_call(flush, out_shape=(jax.ShapeDtypeStruct((LEV, 8, 512), F32)...  0.99 us

profile of v4, /device:TPU:6, one launch (start us, length us, event | category | flops | bytes accessed | tf_op | source)
XLA Modules:
  0.0 30.0 jit_solution(2702569243506082626)
XLA Ops:
  0.6 28.4 %window.1 = (f32[64,8,512]{2,1,0:T(8,128)S(1)}, f32[4,8,512]{2,1,0:T(8,128)S(1)}) custom-call(f32[64,8,512]{2,1,0:T(8,128)} %state_h.1, f32[63,8,512]{2,1,0:T(8,128)} %vert_h.1, f32[8,512]{1,0:T(8,128)} %nu_h.1, s32[8,512]{1,0:T(8,128)} %mask_h.1, f32[4,8,512]{2,1,0:T(8,128)} %coup_h.1, f32[4,8,512]{2,1,0:T(8,128)} %surf_h.1, bf16[32,4,128,128]{3,2,1,0:T(8,128)(2,1)} %w_h.1, ...), custom_call_target="tpu_custom_call" | custom-call | tf_op jit(solution)/shard_map/window/pallas_call | solution.py:625
  29.0 1.0 %flush.1 = (f32[64,8,512]{2,1,0:T(8,128)}, f32[4,8,512]{2,1,0:T(8,128)}) custom-call(f32[64,8,512]{2,1,0:T(8,128)S(1)} %get-tuple-element.4.state_v, f32[4,8,512]{2,1,0:T(8,128)S(1)} %get-tuple-element.5.received_v), custom_call_target="tpu_custom_call" | custom-call | tf_op jit(solution)/shard_map/flush/pallas_call | solution.py:638

commit v5 on v4

--- a/solution.py
+++ b/solution.py
@@ -22,6 +22,7 @@
 WCH = 8
 HR = 3 * LEV + 8
 GAIN = 0.25
+OUT = 4
 
 
 def iota(shape, dim):
@@ -39,10 +40,10 @@
 
 def kernel(
     state_h, vert_h, nu_h, mask_h, coup_h, surf_h, w_h, dt_h, db_h, dg_h,
-    out_h, rec_h,
+    ru_fwd, inv, ww, ends, rec_h,
     w_v, s0, st, ve, nu, mask, coup, surf, dt, db, dg,
     xs, terms, slab, got, ps, xr, es, xe,
-    se, re, xh, coef, coef_h, wet, inv, ww, mid, rg, ru_fwd, uu, gg,
+    se, re, xh, coef, coef_h, wet, mid, rg, uu, gg,
     lsem, wsem, ssem, rsem, hs, hr, xss, xrs, ess, ers,
 ):
     grp = lax.axis_index("grp")
@@ -214,7 +215,7 @@
 
     @pl.loop(1, TILES)
     def _(d):
-        a2a(d).start()
+        a2a((d * 13) % TILES).start()
 
     edge = [halo(side) for side in range(2)]
     to_above, to_below = (dev != 0) & (dev != 96), (dev != 127) & (dev != 95)
@@ -544,58 +545,63 @@
             n_b.append(ww[c, l_b] * s)
         return n_t, n_b
 
-    r_t, _ = lax.fori_loop(0, HALF, second, (forc, zeros), unroll=4)
-    x_t, x_b = [], []
+    r_t, _ = lax.fori_loop(0, HALF, second, (forc, zeros), unroll=8)
     for c in range(CB):
         x32 = (ru_fwd[c, HALF] + r_t[c]) * mid[c]
-        x_t.append(x32)
-        x_b.append(inv[c, HALF - 1] * ru_fwd[c, HALF - 1] + ww[c, HALF - 1] * x32)
-
-    def back2(i, carry):
+        ends[0, c] = x32
+        ends[1, c] = inv[c, HALF - 1] * ru_fwd[c, HALF - 1] + ww[c, HALF - 1] * x32
+
+    @pl.when(to_above)
+    def _():
+        edge[0].wait_send()
+
+    @pl.when(to_below)
+    def _():
+        edge[1].wait_send()
+
+
+    @pl.loop(1, TILES)
+    def _(d):
+        a2a(d).wait_send()
+
+    @pl.when(ocean)
+    def _():
+        for d in ocean_sends():
+            d.wait_send()
+
+    @pl.when(jnp.logical_not(ocean))
+    def _():
+        for d in air_sends():
+            d.wait_send()
+
+
+def finish(fwd, inv, ww, ends, received_v, state_h, received_h, out, sem):
+    copies = [pltpu.make_async_copy(received_v, received_h, sem.at[0])]
+    copies[0].start()
+    step = HALF // OUT
+
+    def back(i, carry):
         x_t, x_b = carry
         l_t, l_b = HALF - 1 - i, HALF + i
         n_t, n_b = [], []
         for c in range(CB):
-            x0 = inv[c, l_t] * ru_fwd[c, l_t] + ww[c, l_t] * x_t[c]
-            x1 = inv[c, l_b] * ru_fwd[c, l_b] + ww[c, l_b] * x_b[c]
-            out_h[l_t, :, c * 128:(c + 1) * 128] = x0
-            out_h[l_b, :, c * 128:(c + 1) * 128] = x1
+            cs = slice(c * 128, (c + 1) * 128)
+            x0 = inv[c, l_t] * fwd[c, l_t] + ww[c, l_t] * x_t[c]
+            x1 = inv[c, l_b] * fwd[c, l_b] + ww[c, l_b] * x_b[c]
+            out[l_t, :, cs] = x0
+            out[l_b, :, cs] = x1
             n_t.append(x0)
             n_b.append(x1)
         return n_t, n_b
 
-    lax.fori_loop(0, HALF, back2, (x_t, x_b), unroll=8)
-    @pl.when(to_above)
-    def _():
-        edge[0].wait_send()
-
-    @pl.when(to_below)
-    def _():
-        edge[1].wait_send()
-
-
-    @pl.loop(1, TILES)
-    def _(d):
-        a2a(d).wait_send()
-
-    @pl.when(ocean)
-    def _():
-        for d in ocean_sends():
-            d.wait_send()
-
-    @pl.when(jnp.logical_not(ocean))
-    def _():
-        for d in air_sends():
-            d.wait_send()
-
-
-def flush(state_v, received_v, state_h, received_h, sem):
-    copies = [
-        pltpu.make_async_copy(state_v, state_h, sem.at[0]),
-        pltpu.make_async_copy(received_v, received_h, sem.at[1]),
-    ]
-    for d in copies:
-        d.start()
+    carry = ([ends[0, c] for c in range(CB)], [ends[1, c] for c in range(CB)])
+    for j in range(OUT):
+        carry = lax.fori_loop(j * step, (j + 1) * step, back, carry, unroll=step)
+        for half, first in enumerate((HALF - (j + 1) * step, HALF + j * step)):
+            rows = pl.ds(first, step)
+            d = pltpu.make_async_copy(out.at[rows], state_h.at[rows], sem.at[1 + 2 * j + half])
+            d.start()
+            copies.append(d)
     for d in copies:
         d.wait()
 
@@ -615,8 +621,8 @@
         vm((3, 2, 8, 128), F32), vm((3, 2, 8, 128), F32),
         vm((2, CB, HR, 128), F32), vm((2, CB, HR, 128), F32), vm((LEV, 8, 128), F32),
         vm((5, CB, 8, 128), F32), vm((5, 8, 128), F32), vm((CB, 8, 128), F32),
-        vm(five, F32), vm(five, F32), vm((CB, 8, 128), F32),
-        vm((CB + 1, HALF, 8, 128), F32), vm(five, F32), vm(five, F32), vm(five, F32),
+        vm((CB, 8, 128), F32),
+        vm((CB + 1, HALF, 8, 128), F32), vm(five, F32), vm(five, F32),
         dma((16,)), dma((WCH,)), dma((TILES,)), dma((TILES,)), dma((2,)), dma((2,)),
         dma((3,)), dma((3,)), dma((3, 2)), dma((3, 2)),
     ]
@@ -625,10 +631,11 @@
     outs = pl.pallas_call(
         kernel,
         out_shape=(
-            vm((LEV, 8, 512), F32), vm((F, 8, 512), F32),
+            vm(five, F32), vm(five, F32), vm(five, F32), vm((2, CB, 8, 128), F32),
+            vm((F, 8, 512), F32),
         ),
         in_specs=[hbm] * 10,
-        out_specs=(out, out),
+        out_specs=(out,) * 5,
         scratch_shapes=scratch,
         compiler_params=pltpu.CompilerParams(
             collective_id=0, has_side_effects=True, vmem_limit_bytes=50 * 1024 * 1024
@@ -636,14 +643,15 @@
         name="window",
     )(*(pltpu.with_memory_space_constraint(a, pltpu.HBM) for a in (*args[:7], *(a.T for a in args[7:]))))
     return pl.pallas_call(
-        flush,
+        finish,
         out_shape=(
             jax.ShapeDtypeStruct((LEV, 8, 512), F32), jax.ShapeDtypeStruct((F, 8, 512), F32),
         ),
-        in_specs=[pl.BlockSpec(memory_space=pltpu.VMEM)] * 2,
+        in_specs=[pl.BlockSpec(memory_space=pltpu.VMEM)] * 5,
         out_specs=(hbm, hbm),
-        scratch_shapes=[dma((2,))],
-        name="flush",
+        scratch_shapes=[vm((LEV, 8, 512), F32), dma((1 + 2 * OUT,))],
+        compiler_params=pltpu.CompilerParams(vmem_limit_bytes=16 * 1024 * 1024),
+        name="finish",
     )(*(pltpu.with_memory_space_constraint(a, pltpu.VMEM) for a in outs))
 
 

time: 30.1 us -> 29.5 us (0.980)
  Pallas kernels: 29.4 us -> 28.6 us
    pallas_call x2, Pallas kernels: 29.4 us -> 28.6 us  [the longest x1 27.5 us: local(): pl.pallas_call(kernel, out_shape=(vm(five, F32), vm(five, F32), vm(five,...]
where the time goes in v5:
time: 29.5 us; the launch traced here: 29.2 us
  Pallas kernels  28.6 us (97%)
  between operations  0.64 us (2%)
    pallas_call x1, Pallas kernels, local(): pl.pallas_call(kernel, out_shape=(vm(five, F32), vm(five, F32), vm(five,...  27.5 us
    pallas_call x1, Pallas kernels, local(): pl.pallas_call(finish, out_shape=(jax.ShapeDtypeStruct((LEV, 8, 512), F32...  1.08 us

profile of v5, /device:TPU:6, one launch (start us, length us, event | category | flops | bytes accessed | tf_op | source)
XLA Modules:
  0.0 29.2 jit_solution(9717853694002412439)
XLA Ops:
  0.6 27.5 %window.1 = (f32[5,64,8,128]{3,2,1,0:T(8,128)S(1)}, f32[5,64,8,128]{3,2,1,0:T(8,128)S(1)}, f32[5,64,8,128]{3,2,1,0:T(8,128)S(1)}, f32[2,4,8,128]{3,2,1,0:T(8,128)S(1)}, f32[4,8,512]{2,1,0:T(8,128)S(1)}) custom-call(f32[64,8,512]{2,1,0:T(8,128)} %state_h.1, f32[63,8,512]{2,1,0:T(8,128)} %vert_h.1, f32[8,512]{1,0:T(8,128)} %nu_h.1, s32[8,512]{1,0:T(8,128)} %mask_h.1, ...), custom_call_target="tpu_custom_call" | custom-call | tf_op jit(solution)/shard_map/window/pallas_call | solution.py:631
  28.2 1.1 %finish.1 = (f32[64,8,512]{2,1,0:T(8,128)}, f32[4,8,512]{2,1,0:T(8,128)}) custom-call(f32[5,64,8,128]{3,2,1,0:T(8,128)S(1)} %get-tuple-element.7.fwd, f32[5,64,8,128]{3,2,1,0:T(8,128)S(1)} %get-tuple-element.8.inv, f32[5,64,8,128]{3,2,1,0:T(8,128)S(1)} %get-tuple-element.9.ww, f32[2,4,8,128]{3,2,1,0:T(8,128)S(1)} %get-tuple-element.10.ends, ...), custom_call_target="tpu_custom_call" | custom-call | tf_op jit(solution)/shard_map/finish/pallas_call | solution.py:645

commit v6 on v5

--- a/solution.py
+++ b/solution.py
@@ -19,7 +19,7 @@
 MSG = 40
 SENT = 33
 CB = 4
-WCH = 8
+WCH = 4
 HR = 3 * LEV + 8
 GAIN = 0.25
 OUT = 4
@@ -213,19 +213,27 @@
     def _():
         pl.semaphore_wait(barrier, 31 + 2 + 3)
 
+    edge = [halo(side) for side in range(2)]
+    to_above, to_below = (dev != 0) & (dev != 96), (dev != 127) & (dev != 95)
+    from_above, from_below = (dev != 0) & (dev != 96), (dev != 127) & (dev != 95)
+
+    @pl.when(to_above & (tile == 0))
+    def _():
+        edge[0].start()
+
+    @pl.when(to_below & (tile == TILES - 1))
+    def _():
+        edge[1].start()
+
     @pl.loop(1, TILES)
     def _(d):
         a2a((d * 13) % TILES).start()
 
-    edge = [halo(side) for side in range(2)]
-    to_above, to_below = (dev != 0) & (dev != 96), (dev != 127) & (dev != 95)
-    from_above, from_below = (dev != 0) & (dev != 96), (dev != 127) & (dev != 95)
-
-    @pl.when(to_above)
+    @pl.when(tile != 0)
     def _():
         edge[0].start()
 
-    @pl.when(to_below)
+    @pl.when(tile != TILES - 1)
     def _():
         edge[1].start()
 
@@ -327,7 +335,7 @@
 
     def ocean_sends():
         copies = []
-        for g in range(3):
+        for g in (1, 0, 2):
             copies.append(across_edge(g, 0, dev_id((g * TILES + tile + 95) % 96), 0))
             copies.append(across_edge(g, 1, dev_id((g * TILES + tile + 1) % 96), 0))
             copies.append(across(g, ps.at[g], (g, tile), 0))

time: 29.5 us -> 29.3 us (level)
  no operation moved by 1% of the time
where the time goes in v6:
time: 29.3 us; the launch traced here: 29.2 us
  Pallas kernels  28.6 us (98%)
  between operations  0.64 us (2%)
    pallas_call x1, Pallas kernels, local(): pl.pallas_call(kernel, out_shape=(vm(five, F32), vm(five, F32), vm(five,...  27.5 us
    pallas_call x1, Pallas kernels, local(): pl.pallas_call(finish, out_shape=(jax.ShapeDtypeStruct((LEV, 8, 512), F32...  1.08 us

profile of v6, /device:TPU:6, one launch (start us, length us, event | category | flops | bytes accessed | tf_op | source)
XLA Modules:
  0.0 29.2 jit_solution(18056745490400559551)
XLA Ops:
  0.6 27.5 %window.1 = (f32[5,64,8,128]{3,2,1,0:T(8,128)S(1)}, f32[5,64,8,128]{3,2,1,0:T(8,128)S(1)}, f32[5,64,8,128]{3,2,1,0:T(8,128)S(1)}, f32[2,4,8,128]{3,2,1,0:T(8,128)S(1)}, f32[4,8,512]{2,1,0:T(8,128)S(1)}) custom-call(f32[64,8,512]{2,1,0:T(8,128)} %state_h.1, f32[63,8,512]{2,1,0:T(8,128)} %vert_h.1, f32[8,512]{1,0:T(8,128)} %nu_h.1, s32[8,512]{1,0:T(8,128)} %mask_h.1, ...), custom_call_target="tpu_custom_call" | custom-call | tf_op jit(solution)/shard_map/window/pallas_call | solution.py:639
  28.1 1.1 %finish.1 = (f32[64,8,512]{2,1,0:T(8,128)}, f32[4,8,512]{2,1,0:T(8,128)}) custom-call(f32[5,64,8,128]{3,2,1,0:T(8,128)S(1)} %get-tuple-element.7.fwd, f32[5,64,8,128]{3,2,1,0:T(8,128)S(1)} %get-tuple-element.8.inv, f32[5,64,8,128]{3,2,1,0:T(8,128)S(1)} %get-tuple-element.9.ww, f32[2,4,8,128]{3,2,1,0:T(8,128)S(1)} %get-tuple-element.10.ends, ...), custom_call_target="tpu_custom_call" | custom-call | tf_op jit(solution)/shard_map/finish/pallas_call | solution.py:653
